TPU v7x, 32 devices: a whole 2x2x4 slice. The times are simulated.
32 devices in a mesh: ha: 16 (over z, x, core), col: 2 (over y).
Axes of the slice: x: 2, y: 2, z: 4, core: 2. Of those that a mesh axis runs over, the one named last changes fastest.
Arguments:
- input_a: bfloat16 [1, 16, 48, 512], P(None, 'ha', None, 'col'), may hold values from -6 to 6
- input_b: bfloat16 [1, 16, 72, 512], P(None, 'ha', None, 'col'), may hold values from -6 to 6
- skip_a: bfloat16 [1, 32, 96, 512], P(None, 'ha', None, 'col'), may hold values from -6 to 6
- skip_b: bfloat16 [1, 32, 144, 512], P(None, 'ha', None, 'col'), may hold values from -6 to 6
- labels_a: int32 [1, 32, 96], P(None, 'ha'), may hold values from 0 to 1
- labels_b: int32 [1, 32, 144], P(None, 'ha'), may hold values from 0 to 1
- valid_a: int32 [1, 32, 96], P(None, 'ha'), may hold values from 0 to 1
- valid_b: int32 [1, 32, 144], P(None, 'ha'), may hold values from 0 to 1
- w_enter: float32 [3, 3, 512, 1024], P(None, None, 'ha', 'col'), may hold values from -0.09375 to 0.09375
- moment_enter: float32 [3, 3, 512, 1024], P(None, None, 'ha', 'col'), may hold values from -0.00010681152 to 0.00010681152
- square_enter: float32 [3, 3, 512, 1024], P(None, None, 'ha', 'col'), may hold values from 2.1152344e-10 to 8.4609375e-10
- w_middle: float32 [3, 3, 1024, 1024], P(None, None, 'ha', 'col'), may hold values from -0.0625 to 0.0625
- moment_middle: float32 [3, 3, 1024, 1024], P(None, None, 'ha', 'col'), may hold values from -0.00010681152 to 0.00010681152
- square_middle: float32 [3, 3, 1024, 1024], P(None, None, 'ha', 'col'), may hold values from 2.1152344e-10 to 8.4609375e-10
- w_upward: float32 [2, 2, 1024, 512], P(None, None, 'ha', 'col'), may hold values from -0.1875 to 0.1875
- moment_upward: float32 [2, 2, 1024, 512], P(None, None, 'ha', 'col'), may hold values from -0.00012207031 to 0.00012207031
- square_upward: float32 [2, 2, 1024, 512], P(None, None, 'ha', 'col'), may hold values from 3.2819011e-10 to 1.3127605e-09
- w_merge: float32 [3, 3, 1024, 512], P(None, None, 'ha', 'col'), may hold values from -0.0625 to 0.0625
- moment_merge: float32 [3, 3, 1024, 512], P(None, None, 'ha', 'col'), may hold values from -0.00036621094 to 0.00036621094
- square_merge: float32 [3, 3, 1024, 512], P(None, None, 'ha', 'col'), may hold values from 2.8710938e-09 to 1.1484375e-08
- w_head: float32 [512, 2], P('col'), may hold values from -0.5 to 0.5
- moment_head: float32 [512, 2], P('col'), may hold values from -0.02734375 to 0.02734375
- square_head: float32 [512, 2], P('col'), may hold values from 6.510417e-06 to 0.00026041668
Outputs:
- enter_master: float32 [3, 3, 512, 1024], P(None, None, 'ha', 'col')
- enter_moment: float32 [3, 3, 512, 1024], P(None, None, 'ha', 'col')
- enter_square: float32 [3, 3, 512, 1024], P(None, None, 'ha', 'col')
- enter_copy: bfloat16 [3, 3, 512, 1024], P(None, None, 'ha', 'col')
- middle_master: float32 [3, 3, 1024, 1024], P(None, None, 'ha', 'col')
- middle_moment: float32 [3, 3, 1024, 1024], P(None, None, 'ha', 'col')
- middle_square: float32 [3, 3, 1024, 1024], P(None, None, 'ha', 'col')
- middle_copy: bfloat16 [3, 3, 1024, 1024], P(None, None, 'ha', 'col')
- upward_master: float32 [2, 2, 1024, 512], P(None, None, 'ha', 'col')
- upward_moment: float32 [2, 2, 1024, 512], P(None, None, 'ha', 'col')
- upward_square: float32 [2, 2, 1024, 512], P(None, None, 'ha', 'col')
- upward_copy: bfloat16 [2, 2, 1024, 512], P(None, None, 'ha', 'col')
- merge_master: float32 [3, 3, 1024, 512], P(None, None, 'ha', 'col')
- merge_moment: float32 [3, 3, 1024, 512], P(None, None, 'ha', 'col')
- merge_square: float32 [3, 3, 1024, 512], P(None, None, 'ha', 'col')
- merge_copy: bfloat16 [3, 3, 1024, 512], P(None, None, 'ha', 'col')
- head_master: float32 [512, 2], P('col')
- head_moment: float32 [512, 2], P('col')
- head_square: float32 [512, 2], P('col')
- head_copy: bfloat16 [512, 2], P('col')
- loss_sum: float32 [], replicated
- label_total: float32 [], replicated
All inputs are finite; a program needn't handle non-finite values.
Results may differ from a plain program's by a relative error of at most 0.025.
Values may be sent and summed in bfloat16 or wider, within the bound.
A program may use at most 192 MiB of HBM per device.

v0:
```python
import jax
import jax.numpy as jnp
from jax import lax
from jax.sharding import PartitionSpec as P

STEP = 10


NUMBERS = ("NHWC", "HWIO", "NHWC")
BETA_ONE = 0.9
BETA_TWO = 0.95
RATE = 0.08
DECAY = 0.1
EPSILON = 1e-08


def extended(cells, sides, width):
    for axis, dim in sides:
        count = lax.axis_size(axis)
        ends = count - 1
        head = lax.slice_in_dim(cells, 0, width, axis=dim)
        tail = lax.slice_in_dim(cells, cells.shape[dim] - width, cells.shape[dim], axis=dim)
        cells = jnp.concatenate(
            [
                lax.ppermute(tail, axis, [(i, (i + 1) % count) for i in range(ends)]),
                cells,
                lax.ppermute(head, axis, [((i + 1) % count, i) for i in range(ends)]),
            ],
            axis=dim,
        )
    return cells


def shortened(value):

    def short(part):
        return part.astype(jnp.bfloat16) if part.dtype == jnp.float32 else part

    return jax.tree.map(short, value)


def convolve_rows(padded, weight):
    return lax.conv_general_dilated(
        padded,
        weight,
        (1, 1),
        ((0, 0), (1, 1)),
        dimension_numbers=NUMBERS,
        preferred_element_type=jnp.float32,
    )


def flipped(weight):
    return jnp.transpose(weight[::-1, ::-1], (0, 1, 3, 2))


def upsample(values, weight):
    product = jnp.einsum("nhwc,abcd->nhawbd", values, weight, preferred_element_type=jnp.float32)
    return product.reshape(
        product.shape[0], 2 * product.shape[1], 2 * product.shape[3], product.shape[5]
    )


def split_pixels(upstream):
    return upstream.reshape(
        upstream.shape[0], upstream.shape[1] // 2, 2, upstream.shape[2] // 2, 2, upstream.shape[3]
    )


def upsample_back(upstream, weight):
    return jnp.einsum(
        "nhawbd,abcd->nhwc", split_pixels(upstream), weight, preferred_element_type=jnp.float32
    )


def upsample_weight(values, upstream):
    return jnp.einsum(
        "nhwc,nhawbd->abcd", values, split_pixels(upstream), preferred_element_type=jnp.float32
    )


def tap_grads(padded, upstream):
    wide = jnp.pad(padded, ((0, 0), (0, 0), (1, 1), (0, 0)))
    height, across = (upstream.shape[1], upstream.shape[2])
    stacked = []
    for row_tap in range(3):
        tapline = []
        for col_tap in range(3):
            window = wide[:, row_tap : row_tap + height, col_tap : col_tap + across, :]
            tapline.append(
                jnp.einsum("nhwc,nhwd->cd", window, upstream, preferred_element_type=jnp.float32)
            )
        stacked.append(jnp.stack(tapline))
    return jnp.stack(stacked)


def alternate(weight, groups):
    dims = weight.shape
    shaped = weight.reshape(dims[0], dims[1], 2, groups, dims[2] // (2 * groups), dims[3])
    return shaped.transpose(0, 1, 3, 2, 4, 5).reshape(dims)


def deinterleave(weight, groups):
    dims = weight.shape
    shaped = weight.reshape(dims[0], dims[1], groups, 2, dims[2] // (2 * groups), dims[3])
    return shaped.transpose(0, 1, 3, 2, 4, 5).reshape(dims)


def gelu_back(pre_act, upstream):
    return jax.vjp(jax.nn.gelu, pre_act)[1](upstream)[0]


def focal(logits, labels, usable):
    logprob = jax.nn.log_softmax(logits, axis=-1)
    picked = jnp.where(labels == 1, logprob[..., 1], logprob[..., 0])
    chance = jnp.exp(picked)
    return jnp.sum(usable.astype(jnp.float32) * (-((1.0 - chance) ** 2) * picked))


def loss_terms(logits, labels, usable, labelled):
    running, pull = jax.vjp(lambda values: focal(values, labels, usable), logits)
    return (running, pull(1.0 / labelled)[0])


def gather_channels(values):
    return lax.all_gather(values, "col", axis=3, tiled=True)


def spread_back(partial_value):
    return lax.psum_scatter(partial_value, "col", scatter_dimension=3, tiled=True)


def conv_forward(local, weight):
    padded = extended(local, (("ha", 1),), 1)
    whole = gather_channels(padded)
    return (convolve_rows(whole, weight), whole)


def up_forward(local, weight):
    whole = gather_channels(local)
    return (upsample(whole, weight), whole)


def conv_weight_grad(kept, upstream):
    return tap_grads(kept, upstream)


def up_weight_grad(kept, upstream):
    return upsample_weight(kept, upstream)


def backward_weights(merge_up, upward, middle):
    return (flipped(merge_up), upward, flipped(middle))


def conv_input_grad(back_weight, upstream):
    padded = extended(shortened(upstream), (("ha", 1),), 1).astype(upstream.dtype)
    return spread_back(convolve_rows(padded, back_weight))


def up_input_grad(back_weight, upstream):
    return spread_back(upsample_back(upstream, back_weight))


def forward_pass(picture, skipped, copies):
    enter, middle, upward, merge_mixed, back_merge, back_upward, back_middle, head_copy = copies
    pre_one, kept_one = conv_forward(picture, enter)
    act_one = jax.nn.gelu(pre_one).astype(jnp.bfloat16)
    pre_two, kept_two = conv_forward(act_one, middle)
    act_two = jax.nn.gelu(pre_two).astype(jnp.bfloat16)
    raised, kept_up = up_forward(act_two, upward)
    joined = jnp.concatenate([raised.astype(jnp.bfloat16), skipped], axis=3)
    pre_three, kept_three = conv_forward(joined, merge_mixed)
    act_three = jax.nn.gelu(pre_three).astype(jnp.bfloat16)
    partial_value = jnp.einsum(
        "nhwc,ck->nhwk", act_three, head_copy, preferred_element_type=jnp.float32
    )
    return (
        partial_value,
        (pre_one, kept_one, pre_two, kept_two, kept_up, pre_three, kept_three, act_three),
    )


def backward_pass(saved, dlogits, copies):
    enter, middle, upward, merge_mixed, back_merge, back_upward, back_middle, head_copy = copies
    pre_one, kept_one, pre_two, kept_two, kept_up, pre_three, kept_three, act_three = saved
    back_three = jnp.einsum("nhwk,ck->nhwc", dlogits, head_copy, preferred_element_type=jnp.float32)
    grad_head = jnp.einsum("nhwc,nhwk->ck", act_three, dlogits, preferred_element_type=jnp.float32)
    grad_three = gelu_back(pre_three, back_three).astype(jnp.bfloat16)
    grad_merge = conv_weight_grad(kept_three, grad_three)
    d_raised = conv_input_grad(back_merge, grad_three).astype(jnp.bfloat16)
    grad_upward = up_weight_grad(kept_up, d_raised)
    back_two = up_input_grad(back_upward, d_raised)
    grad_two = gelu_back(pre_two, back_two).astype(jnp.bfloat16)
    grad_middle = conv_weight_grad(kept_two, grad_two)
    back_one = conv_input_grad(back_middle, grad_two)
    grad_one = gelu_back(pre_one, back_one).astype(jnp.bfloat16)
    grad_enter = conv_weight_grad(kept_one, grad_one)
    return (grad_enter, grad_middle, grad_upward, grad_merge, grad_head)


def adamw(master, moment, square, gradient):
    moment_new = BETA_ONE * moment + (1.0 - BETA_ONE) * gradient
    square_new = BETA_TWO * square + (1.0 - BETA_TWO) * gradient * gradient
    fixed_moment = moment_new / (1.0 - BETA_ONE**STEP)
    fixed_square = square_new / (1.0 - BETA_TWO**STEP)
    master_new = master - RATE * (
        fixed_moment / (jnp.sqrt(fixed_square) + EPSILON) + DECAY * master
    )
    return (master_new, moment_new, square_new, master_new.astype(jnp.bfloat16))


def own_rows(summed, local):
    return lax.dynamic_slice_in_dim(
        summed, lax.axis_index("ha") * local.shape[2], local.shape[2], 2
    )


def body(
    input_a,
    input_b,
    skip_a,
    skip_b,
    labels_a,
    labels_b,
    valid_a,
    valid_b,
    w_enter,
    moment_enter,
    square_enter,
    w_middle,
    moment_middle,
    square_middle,
    w_upward,
    moment_upward,
    square_upward,
    w_merge,
    moment_merge,
    square_merge,
    w_head,
    moment_head,
    square_head,
):
    groups = lax.axis_size("col")
    enter, middle, upward, merge = (
        lax.all_gather(w_enter.astype(jnp.bfloat16), "ha", axis=2, tiled=True),
        lax.all_gather(w_middle.astype(jnp.bfloat16), "ha", axis=2, tiled=True),
        lax.all_gather(w_upward.astype(jnp.bfloat16), "ha", axis=2, tiled=True),
        lax.all_gather(w_merge.astype(jnp.bfloat16), "ha", axis=2, tiled=True),
    )
    head_low = w_head.astype(jnp.bfloat16)
    merge_up = merge[:, :, : merge.shape[2] // 2]
    back_merge, back_upward, back_middle = backward_weights(merge_up, upward, middle)
    copies = (
        enter,
        middle,
        upward,
        alternate(merge, groups),
        back_merge,
        back_upward,
        back_middle,
        head_low,
    )
    labelled = lax.psum(
        jnp.sum(valid_a.astype(jnp.float32)) + jnp.sum(valid_b.astype(jnp.float32)), "ha"
    )
    partial_a, saved_a = forward_pass(input_a, skip_a, copies)
    partial_b, saved_b = forward_pass(input_b, skip_b, copies)
    logits_a, logits_b = lax.psum((partial_a, partial_b), "col")
    loss_a, dlogits_a = loss_terms(logits_a, labels_a, valid_a, labelled)
    loss_b, dlogits_b = loss_terms(logits_b, labels_b, valid_b, labelled)
    grads_a = backward_pass(saved_a, dlogits_a.astype(jnp.bfloat16), copies)
    grads_b = backward_pass(saved_b, dlogits_b.astype(jnp.bfloat16), copies)
    local_enter = grads_a[0] + grads_b[0]
    local_middle = grads_a[1] + grads_b[1]
    local_upward = grads_a[2] + grads_b[2]
    local_merge = deinterleave(grads_a[3] + grads_b[3], groups)
    local_head = grads_a[4] + grads_b[4]
    local_loss = loss_a + loss_b
    full_enter, full_middle, full_upward, full_merge, head_total, loss_total = (
        lax.psum(local_enter.astype(jnp.bfloat16), "ha").astype(jnp.float32),
        lax.psum(local_middle.astype(jnp.bfloat16), "ha").astype(jnp.float32),
        lax.psum(local_upward.astype(jnp.bfloat16), "ha").astype(jnp.float32),
        lax.psum(local_merge.astype(jnp.bfloat16), "ha").astype(jnp.float32),
        lax.psum(local_head.astype(jnp.bfloat16), "ha").astype(jnp.float32),
        lax.psum(local_loss.astype(jnp.bfloat16), "ha").astype(jnp.float32),
    )
    grad_enter = own_rows(full_enter, w_enter)
    grad_middle = own_rows(full_middle, w_middle)
    grad_upward = own_rows(full_upward, w_upward)
    grad_merge = own_rows(full_merge, w_merge)
    enter_out = adamw(w_enter, moment_enter, square_enter, grad_enter)
    middle_out = adamw(w_middle, moment_middle, square_middle, grad_middle)
    upward_out = adamw(w_upward, moment_upward, square_upward, grad_upward)
    merge_out = adamw(w_merge, moment_merge, square_merge, grad_merge)
    head_out = adamw(w_head, moment_head, square_head, head_total)
    return (
        enter_out[0],
        enter_out[1],
        enter_out[2],
        enter_out[3],
        middle_out[0],
        middle_out[1],
        middle_out[2],
        middle_out[3],
        upward_out[0],
        upward_out[1],
        upward_out[2],
        upward_out[3],
        merge_out[0],
        merge_out[1],
        merge_out[2],
        merge_out[3],
        head_out[0],
        head_out[1],
        head_out[2],
        head_out[3],
        loss_total,
        labelled,
    )


def solution(mesh):
    placed = (
        P(None, "ha", None, "col"),
        P(None, "ha", None, "col"),
        P(None, "ha", None, "col"),
        P(None, "ha", None, "col"),
        P(None, "ha", None),
        P(None, "ha", None),
        P(None, "ha", None),
        P(None, "ha", None),
        P(None, None, "ha", "col"),
        P(None, None, "ha", "col"),
        P(None, None, "ha", "col"),
        P(None, None, "ha", "col"),
        P(None, None, "ha", "col"),
        P(None, None, "ha", "col"),
        P(None, None, "ha", "col"),
        P(None, None, "ha", "col"),
        P(None, None, "ha", "col"),
        P(None, None, "ha", "col"),
        P(None, None, "ha", "col"),
        P(None, None, "ha", "col"),
        P("col", None),
        P("col", None),
        P("col", None),
    )
    return jax.shard_map(
        body,
        mesh=mesh,
        in_specs=placed,
        out_specs=(
            P(None, None, "ha", "col"),
            P(None, None, "ha", "col"),
            P(None, None, "ha", "col"),
            P(None, None, "ha", "col"),
            P(None, None, "ha", "col"),
            P(None, None, "ha", "col"),
            P(None, None, "ha", "col"),
            P(None, None, "ha", "col"),
            P(None, None, "ha", "col"),
            P(None, None, "ha", "col"),
            P(None, None, "ha", "col"),
            P(None, None, "ha", "col"),
            P(None, None, "ha", "col"),
            P(None, None, "ha", "col"),
            P(None, None, "ha", "col"),
            P(None, None, "ha", "col"),
            P("col", None),
            P("col", None),
            P("col", None),
            P("col", None),
            P(),
            P(),
        ),
        check_vma=False,
    )
```

profile of v0, /device:TPU:14, one launch (start us, length us, event | category | flops | bytes accessed | tf_op | source)
XLA Modules:
  0.0 1103.6 jit_solution(8566508098749208426)
XLA Ops:
  23.6 5.0 all_gather.36
  28.9 5.7 all_gather.44
  35.6 28.9 %all-gather.6.cloned.1.call-done = bf16[3,3,512,512]{3,2,1,0:T(8,128)(2,1)} async-done(((bf16[3,3,32,512]{3,2,1,0:T(8,128)(2,1)}), bf16[3,3,512,512]{3,2,1,0:T(8,128)(2,1)}) %all-gather.6.cloned.1.call-update) | async-done | bytes 4718608 | tf_op jit(solution)/shard_map/all_gather | solution.py:246
  64.5 4.1 subtract_multiply_fusion.5
  73.8 4.4 subtract_multiply_fusion.3
  78.3 3.5 collective-permute-start.13
  83.9 5.8 all_gather.38
  90.2 8.5 all_gather.45
  100.1 47.4 %all-gather.8.cloned.1.call-done = bf16[3,3,1024,512]{3,2,1,0:T(8,128)(2,1)} async-done(((bf16[3,3,64,512]{3,2,1,0:T(8,128)(2,1)}), bf16[3,3,1024,512]{3,2,1,0:T(8,128)(2,1)}) %all-gather.8.cloned.1.call-update) | async-done | bytes 9437200 | tf_op jit(solution)/shard_map/all_gather | solution.py:247
  147.5 6.2 subtract_multiply_fusion.4
  153.8 4.8 all_gather.40
  158.5 31.2 %all-gather.10.cloned.1.call-done = bf16[2,2,1024,256]{3,2,1,0:T(8,128)(2,1)} async-done(((bf16[2,2,64,256]{3,2,1,0:T(8,128)(2,1)}), bf16[2,2,1024,256]{3,2,1,0:T(8,128)(2,1)}) %all-gather.10.cloned.1.call-update) | async-done | bytes 2097168 | tf_op jit(solution)/shard_map/all_gather | solution.py:248
  198.4 6.5 subtract_multiply_fusion.2
  206.5 5.2 all_gather.46
  221.5 28.8 %all-gather.12.cloned.1.call-done = bf16[3,3,1024,256]{3,2,1,0:T(8,128)(2,1)} async-done(((bf16[3,3,64,256]{3,2,1,0:T(8,128)(2,1)}), bf16[3,3,1024,256]{3,2,1,0:T(8,128)(2,1)}) %all-gather.12.cloned.1.call-update) | async-done | bytes 4718608 | tf_op jit(solution)/shard_map/all_gather | solution.py:249
  250.3 5.1 copy.374
  272.4 14.5 %all_gather.42 = bf16[1,4,96,1024]{3,1,2,0:T(4,128)(2,1)S(1)} all-gather(bf16[1,4,96,512]{3,1,2,0:T(4,128)(2,1)S(1)} %pad_maximum_fusion.1), channel_id=1, replica_groups=mesh['ha'=16,'col'=2] {'col'}, dimensions={3}, use_global_device_ids=true | all-gather | bytes 1179648 | tf_op jit(solution)/shard_map/all_gather | solution.py:126
  287.5 3.6 multiply_convert_fusion.1
  294.5 4.2 slice_bitcast_fusion.19
  316.5 5.1 subtract_multiply_fusion
  322.6 5.0 all-reduce.10
  332.3 21.1 %psum.64 = f32[]{:T(128)} all-reduce(f32[]{:T(128)S(6)} %add.216), channel_id=1, replica_groups=mesh['ha'=16,'col'=2] {'ha'}, use_global_device_ids=true, to_apply=%region_5.0 | all-reduce | flops 1 | bytes 8 | tf_op jit(solution)/shard_map/psum | solution.py:264
  356.4 4.6 collective-permute-start.7
  367.9 3.6 collective-permute-start.17
  371.5 10.2 collective-permute-start.16
  381.7 6.0 slice_bitcast_fusion.9
  433.5 3.5 reshape.921
  454.2 20.0 %copy.566 = f32[1,2,96,512]{1,2,0,3:T(8,128)} copy(f32[1,2,96,512]{3,1,2,0:T(2,128)S(1)} %slice_bitcast_fusion.13) | data formatting | bytes 786432
  474.2 18.8 %reshape.930 = f32[512,192]{1,0:T(8,128)} reshape(f32[512,1,96,2]{3,2,1,0:T(8,128)} %bitcast.854) | data formatting | bytes 786432
  493.0 8.3 fusion.3
  505.1 7.4 reduce-scatter.19.cloned.1.call-done
  512.6 14.8 %reshape.931 = bf16[256,1,96,2]{3,2,1,0:T(8,128)(2,1)} reshape(f32[256,192]{1,0:T(8,128)} %reduce-scatter.19.cloned.1.call-done) | data formatting | bytes 294912
  527.4 8.0 copy.567
  541.0 20.1 %copy.568 = f32[1,2,144,512]{1,2,0,3:T(8,128)} copy(f32[1,2,144,512]{3,1,2,0:T(2,128)} %slice_bitcast_fusion.3) | data formatting | bytes 1179648
  561.2 23.1 %reshape.932 = f32[512,288]{1,0:T(8,128)} reshape(f32[512,1,144,2]{3,2,1,0:T(8,128)} %bitcast.853) | data formatting | bytes 1179648
  596.5 5.5 maximum_bitcast_fusion
  605.4 12.1 %reshape.933 = bf16[256,1,144,2]{3,2,1,0:T(8,128)(2,1)} reshape(f32[256,288]{1,0:T(8,128)} %reduce-scatter.21.cloned.1.call-done) | data formatting | bytes 442368
  617.5 9.7 copy.569
  627.5 6.6 convolution_select_fusion.1
  636.7 4.4 fusion.10
  641.1 5.8 reduce-scatter.13.cloned.1.call-done
  655.3 6.4 reduce-scatter.15.cloned.1.call-done
  671.2 6.1 maximum_bitcast_fusion.3
  681.0 6.7 convolution_select_fusion
  689.0 17.3 %fusion = bf16[3,3,1024,512]{3,2,1,0:T(8,128)(2,1)} fusion(f32[1,3,1024,512]{3,2,1,0:T(8,128)} %maximum_bitcast_fusion.2, f32[1,3,1024,512]{3,2,1,0:T(8,128)} %get-tuple-element.191, f32[1,3,1024,512]{3,2,1,0:T(8,128)} %get-tuple-element.190, f32[1,3,1024,512]{3,2,1,0:T(8,128)} %maximum_bitcast_fusion.5, f32[1,3,1024,512]{3,2,1,0:T(8,128)} %get-tuple-element.193, ...), kind=kLoop, calls=%fused_computation.1 | loop fusion | flops 28311552 | bytes 47185920 | tf_op jit(solution)/shard_map/convert_element_type | solution.py:282
  721.5 24.4 %all-reduce.11 = (bf16[256,2]{0,1:T(2,128)(2,1)S(1)}, bf16[]{:T(256)}) all-reduce(bf16[256,2]{0,1:T(2,128)(2,1)S(1)} %fusion.33, bf16[]{:T(256)S(6)} %add.255), channel_id=1, replica_groups=mesh['ha'=16,'col'=2] {'ha'}, use_global_device_ids=true, to_apply=%region_21.22 | all-reduce | flops 513 | bytes 2052 | tf_op jit(solution)/shard_map/psum | solution.py:285
  747.9 336.0 %all-reduce.15.cloned.1.call-done = (bf16[3,3,512,512]{3,2,1,0:T(8,128)(2,1)}, bf16[3,3,1024,512]{3,2,1,0:T(8,128)(2,1)}, bf16[2,2,1024,256]{3,2,1,0:T(8,128)(2,1)}, bf16[3,3,1024,256]{3,2,1,0:T(8,128)(2,1)}) async-done(((bf16[3,3,512,512]{3,2,1,0:T(8,128)(2,1)}, bf16[3,3,1024,512]{3,2,1,0:T(8,128)(2,1)}, bf16[2,2,1024,256]{3,2,1,0:T(8,128)(2,1)}, bf16[3,3,1024,256]{3,2,1,0:T(8,128)(2,1)}), ...) | async-done | bytes 20971536 | tf_op jit(solution)/shard_map/psum | solution.py:281
  1084.0 3.9 fusion.378
  (524 shorter events, 233.2 us)
Async XLA Ops:
  7.3 57.3 %all-gather.6.cloned.1.call-start = ((), (), s32[]{:S(2)}) async-start(), calls=%async_computation.6 | async-start | bytes 5013504 | tf_op jit(solution)/shard_map/all_gather | solution.py:246
  9.2 138.3 %all-gather.8.cloned.1.call-start = ((), (), s32[]{:S(2)}) async-start(), calls=%async_computation.7 | async-start | bytes 10027008 | tf_op jit(solution)/shard_map/all_gather | solution.py:247
  11.5 53.1 %copy-start.84 = (pred[8,7]{0,1:T(8,128)(4,1)S(1)}, pred[8,7]{0,1:T(8,128)(4,1)}, u32[]{:S(2)}) copy-start(pred[8,7]{0,1:T(8,128)(4,1)} %constant.208) | copy-start | bytes 172
  11.5 178.3 %all-gather.10.cloned.1.call-start = ((), (), s32[]{:S(2)}) async-start(), calls=%async_computation.8 | async-start | bytes 2228224 | tf_op jit(solution)/shard_map/all_gather | solution.py:248
  12.2 238.1 %all-gather.12.cloned.1.call-start = ((), (), s32[]{:S(2)}) async-start(), calls=%async_computation.9 | async-start | bytes 5013504 | tf_op jit(solution)/shard_map/all_gather | solution.py:249
  13.1 301.1 %all-gather.14.cloned.1.call-start = ((), (), s32[]{:S(2)}) async-start(), calls=%async_computation.12 | async-start | bytes 1769472 | tf_op jit(solution)/shard_map/all_gather | solution.py:126
  13.1 10.4 collective-permute-start.1
  15.0 8.5 collective-permute-start
  17.5 11.4 %collective-permute-start.11 = (bf16[1,1,72,256]{3,2,1,0:T(8,128)(2,1)S(1)}, bf16[1,1,72,256]{3,2,1,0:T(8,128)(2,1)S(1)}, u32[]{:S(2)}, u32[]{:S(2)}) collective-permute-start(bf16[1,1,72,256]{3,2,1,0:T(8,128)(2,1)S(1)} %copy-done.80), channel_id=1, source_target_pairs={{2,0},{4,2},{6,4},{8,6},{10,8},{12,10},{14,12},{16,14},{18,16},{20... | collective-permute-start | bytes 110600 | tf_op jit(solution)/shard_map/ppermute | solution.py:27
  20.6 8.2 collective-permute-start.10
  23.4 168.6 %copy-start.35 = (bf16[1,2,96,256]{3,1,2,0:T(2,128)(2,1)}, bf16[1,2,96,256]{3,1,2,0:T(2,128)(2,1)S(1)}, u32[]{:S(2)}) copy-start(bf16[1,2,96,256]{3,1,2,0:T(2,128)(2,1)S(1)} %copy.371) | copy-start | bytes 294916
  23.5 189.5 %copy-start.23 = (bf16[1,2,144,256]{3,1,2,0:T(2,128)(2,1)}, bf16[1,2,144,256]{3,1,2,0:T(2,128)(2,1)S(1)}, u32[]{:S(2)}) copy-start(bf16[1,2,144,256]{3,1,2,0:T(2,128)(2,1)S(1)} %copy.422) | copy-start | bytes 442372
  35.4 38.4 %copy-start.83 = (pred[8,10]{0,1:T(8,128)(4,1)S(1)}, pred[8,10]{0,1:T(8,128)(4,1)}, u32[]{:S(2)}) copy-start(pred[8,10]{0,1:T(8,128)(4,1)} %constant.213) | copy-start | bytes 244
  68.7 15.2 %collective-permute-start.3 = (bf16[1,1,48,512]{3,2,1,0:T(8,128)(2,1)S(1)}, bf16[1,1,48,512]{3,2,1,0:T(8,128)(2,1)S(1)}, u32[]{:S(2)}, u32[]{:S(2)}) collective-permute-start(bf16[1,1,48,512]{3,2,1,0:T(8,128)(2,1)S(1)} %slice.331), channel_id=1, source_target_pairs={{2,0},{4,2},{6,4},{8,6},{10,8},{12,10},{14,12},{16,14},{18,16},{20... | collective-permute-start | bytes 147464 | tf_op jit(solution)/shard_map/ppermute | solution.py:27
  71.9 11.9 %collective-permute-start.2 = (bf16[1,1,48,512]{3,2,1,0:T(8,128)(2,1)S(1)}, bf16[1,1,48,512]{3,2,1,0:T(8,128)(2,1)S(1)}, u32[]{:S(2)}, u32[]{:S(2)}) collective-permute-start(bf16[1,1,48,512]{3,2,1,0:T(8,128)(2,1)S(1)} %slice.331), channel_id=1, source_target_pairs={{0,2},{2,4},{4,6},{6,8},{8,10},{10,12},{12,14},{14,16},{16,18},{18... | collective-permute-start | bytes 147464 | tf_op jit(solution)/shard_map/ppermute | solution.py:25
  78.3 11.8 %collective-permute-start.13 = (bf16[1,1,72,512]{3,2,1,0:T(8,128)(2,1)S(1)}, bf16[1,1,72,512]{3,2,1,0:T(8,128)(2,1)S(1)}, u32[]{:S(2)}, u32[]{:S(2)}) collective-permute-start(bf16[1,1,72,512]{3,2,1,0:T(8,128)(2,1)S(1)} %slice.363), channel_id=1, source_target_pairs={{2,0},{4,2},{6,4},{8,6},{10,8},{12,10},{14,12},{16,14},{18,16},{20... | collective-permute-start | bytes 221192 | tf_op jit(solution)/shard_map/ppermute | solution.py:27
  81.9 8.3 collective-permute-start.12
  99.4 54.3 %copy-start.8 = (bf16[3,1,8,10,1024]{4,2,3,0,1:T(8,128)(2,1)}, bf16[3,1,8,10,1024]{4,2,3,0,1:T(8,128)(2,1)S(1)}, u32[]{:S(2)}) copy-start(bf16[3,1,8,10,1024]{4,2,3,0,1:T(8,128)(2,1)S(1)} %copy.419) | copy-start | bytes 1474564
  158.5 46.4 %copy-start.33 = (bf16[1,1,48,1024]{3,2,1,0:T(8,128)(2,1)}, bf16[1,1,48,1024]{3,2,1,0:T(8,128)(2,1)S(1)}, u32[]{:S(2)}) copy-start(bf16[1,1,48,1024]{3,2,1,0:T(8,128)(2,1)S(1)} %all_gather.40) | copy-start | bytes 294916
  193.1 74.6 %collective-permute-start.5 = (bf16[1,1,96,512]{3,1,2,0:T(2,128)(2,1)}, bf16[1,1,96,512]{3,1,2,0:T(2,128)(2,1)}, u32[]{:S(2)}, u32[]{:S(2)}) collective-permute-start(bf16[1,1,96,512]{3,1,2,0:T(2,128)(2,1)} %get-tuple-element.155), channel_id=1, source_target_pairs={{2,0},{4,2},{6,4},{8,6},{10,8},{12,10},{14,12},{16,14},{18,16},{20... | collective-permute-start | bytes 294920 | tf_op jit(solution)/shard_map/ppermute | solution.py:27
  196.3 71.3 %collective-permute-start.4 = (bf16[1,1,96,512]{3,1,2,0:T(2,128)(2,1)}, bf16[1,1,96,512]{3,1,2,0:T(2,128)(2,1)}, u32[]{:S(2)}, u32[]{:S(2)}) collective-permute-start(bf16[1,1,96,512]{3,1,2,0:T(2,128)(2,1)} %get-tuple-element.154), channel_id=1, source_target_pairs={{0,2},{2,4},{4,6},{6,8},{8,10},{10,12},{12,14},{14,16},{16,18},{18... | collective-permute-start | bytes 294920 | tf_op jit(solution)/shard_map/ppermute | solution.py:25
  214.4 55.0 %collective-permute-start.15 = (bf16[1,1,144,512]{3,1,2,0:T(2,128)(2,1)}, bf16[1,1,144,512]{3,1,2,0:T(2,128)(2,1)}, u32[]{:S(2)}, u32[]{:S(2)}) collective-permute-start(bf16[1,1,144,512]{3,1,2,0:T(2,128)(2,1)} %get-tuple-element.149), channel_id=1, source_target_pairs={{2,0},{4,2},{6,4},{8,6},{10,8},{12,10},{14,12},{16,14},{18,16},{20... | collective-permute-start | bytes 442376 | tf_op jit(solution)/shard_map/ppermute | solution.py:27
  217.6 51.8 %collective-permute-start.14 = (bf16[1,1,144,512]{3,1,2,0:T(2,128)(2,1)}, bf16[1,1,144,512]{3,1,2,0:T(2,128)(2,1)}, u32[]{:S(2)}, u32[]{:S(2)}) collective-permute-start(bf16[1,1,144,512]{3,1,2,0:T(2,128)(2,1)} %get-tuple-element.148), channel_id=1, source_target_pairs={{0,2},{2,4},{4,6},{6,8},{8,10},{10,12},{12,14},{14,16},{16,18},{18... | collective-permute-start | bytes 442376 | tf_op jit(solution)/shard_map/ppermute | solution.py:25
  269.4 18.1 %copy-start.97 = (pred[8,13]{0,1:T(8,128)(4,1)S(1)}, pred[8,13]{0,1:T(8,128)(4,1)}, u32[]{:S(2)}) copy-start(pred[8,13]{0,1:T(8,128)(4,1)} %constant.209) | copy-start | bytes 316
  272.3 240.2 %reduce-scatter.19.cloned.1.call-start = ((), (), s32[]{:S(2)}) async-start(), calls=%async_computation.15 | async-start | bytes 786432
  294.5 19.6 %copy-start.79 = (bf16[2,1,96,256]{3,0,2,1:T(2,128)(2,1)}, bf16[2,1,96,256]{3,0,2,1:T(2,128)(2,1)S(1)}, u32[]{:S(2)}) copy-start(bf16[2,1,96,256]{3,0,2,1:T(2,128)(2,1)S(1)} %slice.337) | copy-start | bytes 294916
  356.4 95.3 %collective-permute-start.7 = (bf16[1,1,96,256]{3,2,1,0:T(8,128)(2,1)}, bf16[1,1,96,256]{3,2,1,0:T(8,128)(2,1)}, u32[]{:S(2)}, u32[]{:S(2)}) collective-permute-start(bf16[1,1,96,256]{3,2,1,0:T(8,128)(2,1)} %get-tuple-element.175), channel_id=1, source_target_pairs={{2,0},{4,2},{6,4},{8,6},{10,8},{12,10},{14,12},{16,14},{18,16},{20... | collective-permute-start | bytes 147464 | tf_op jit(solution)/shard_map/ppermute | solution.py:27
  361.0 90.7 %collective-permute-start.6 = (bf16[1,1,96,256]{3,2,1,0:T(8,128)(2,1)}, bf16[1,1,96,256]{3,2,1,0:T(8,128)(2,1)}, u32[]{:S(2)}, u32[]{:S(2)}) collective-permute-start(bf16[1,1,96,256]{3,2,1,0:T(8,128)(2,1)} %get-tuple-element.174), channel_id=1, source_target_pairs={{0,2},{2,4},{4,6},{6,8},{8,10},{10,12},{12,14},{14,16},{16,18},{18... | collective-permute-start | bytes 147464 | tf_op jit(solution)/shard_map/ppermute | solution.py:25
  362.9 18.7 %copy-start.3 = (bf16[1,4,144,1024]{3,1,2,0:T(4,128)(2,1)S(1)}, bf16[1,4,144,1024]{3,1,2,0:T(4,128)(2,1)}, u32[]{:S(2)}) copy-start(bf16[1,4,144,1024]{3,1,2,0:T(4,128)(2,1)} %all-gather.14.cloned.1.call-done) | copy-start | bytes 3538948
  367.9 136.0 %collective-permute-start.17 = (bf16[1,1,144,256]{3,2,1,0:T(8,128)(2,1)}, bf16[1,1,144,256]{3,2,1,0:T(8,128)(2,1)S(1)}, u32[]{:S(2)}, u32[]{:S(2)}) collective-permute-start(bf16[1,1,144,256]{3,2,1,0:T(8,128)(2,1)} %get-tuple-element.165), channel_id=1, source_target_pairs={{2,0},{4,2},{6,4},{8,6},{10,8},{12,10},{14,12},{16,14},{18,16},{20... | collective-permute-start | bytes 221192 | tf_op jit(solution)/shard_map/ppermute | solution.py:27
  371.5 132.4 %collective-permute-start.16 = (bf16[1,1,144,256]{3,2,1,0:T(8,128)(2,1)}, bf16[1,1,144,256]{3,2,1,0:T(8,128)(2,1)}, u32[]{:S(2)}, u32[]{:S(2)}) collective-permute-start(bf16[1,1,144,256]{3,2,1,0:T(8,128)(2,1)} %get-tuple-element.164), channel_id=1, source_target_pairs={{0,2},{2,4},{4,6},{6,8},{8,10},{10,12},{12,14},{14,16},{16,18},{18... | collective-permute-start | bytes 221192 | tf_op jit(solution)/shard_map/ppermute | solution.py:25
  492.9 94.1 %reduce-scatter.11.cloned.1.call-start = ((), (), s32[]{:S(2)}) async-start(), calls=%async_computation.10 | async-start | bytes 294912 | tf_op jit(solution)/shard_map/reduce_scatter | solution.py:130
  536.8 68.5 %reduce-scatter.21.cloned.1.call-start = ((), (), s32[]{:S(2)}) async-start(), calls=%async_computation.16 | async-start | bytes 1179648
  561.2 23.2 %copy-start.34 = (bf16[1,1,48,1024]{3,2,1,0:T(8,128)(2,1)S(1)}, bf16[1,1,48,1024]{3,2,1,0:T(8,128)(2,1)}, u32[]{:S(2)}) copy-start(bf16[1,1,48,1024]{3,2,1,0:T(8,128)(2,1)} %copy-done.33) | copy-start | bytes 294916
  584.3 62.6 %reduce-scatter.13.cloned.1.call-start = ((), (), s32[]{:S(2)}) async-start(), calls=%async_computation.11 | async-start | bytes 294912 | tf_op jit(solution)/shard_map/reduce_scatter | solution.py:130
  588.0 39.2 %collective-permute-start.9 = (bf16[1,1,48,512]{3,2,1,0:T(8,128)(2,1)S(1)}, bf16[1,1,48,512]{3,2,1,0:T(8,128)(2,1)S(1)}, u32[]{:S(2)}, u32[]{:S(2)}) collective-permute-start(bf16[1,1,48,512]{3,2,1,0:T(8,128)(2,1)S(1)} %fusion.219), channel_id=1, source_target_pairs={{2,0},{4,2},{6,4},{8,6},{10,8},{12,10},{14,12},{16,14},{18,16},{20... | collective-permute-start | bytes 147464 | tf_op jit(solution)/shard_map/ppermute | solution.py:27
  590.0 37.3 %collective-permute-start.8 = (bf16[1,1,48,512]{3,2,1,0:T(8,128)(2,1)S(1)}, bf16[1,1,48,512]{3,2,1,0:T(8,128)(2,1)S(1)}, u32[]{:S(2)}, u32[]{:S(2)}) collective-permute-start(bf16[1,1,48,512]{3,2,1,0:T(8,128)(2,1)S(1)} %fusion.219), channel_id=1, source_target_pairs={{0,2},{2,4},{4,6},{6,8},{8,10},{10,12},{12,14},{14,16},{16,18},{18... | collective-permute-start | bytes 147464 | tf_op jit(solution)/shard_map/ppermute | solution.py:25
  635.1 26.5 %reduce-scatter.15.cloned.1.call-start = ((), (), s32[]{:S(2)}) async-start(), calls=%async_computation.13 | async-start | bytes 442368 | tf_op jit(solution)/shard_map/reduce_scatter | solution.py:130
  641.1 65.2 %reduce-scatter.17.cloned.1.call-start = ((), (), s32[]{:S(2)}) async-start(), calls=%async_computation.14 | async-start | bytes 442368 | tf_op jit(solution)/shard_map/reduce_scatter | solution.py:130
  662.7 18.0 %collective-permute-start.19 = (bf16[1,1,72,512]{3,2,1,0:T(8,128)(2,1)S(1)}, bf16[1,1,72,512]{3,2,1,0:T(8,128)(2,1)S(1)}, u32[]{:S(2)}, u32[]{:S(2)}) collective-permute-start(bf16[1,1,72,512]{3,2,1,0:T(8,128)(2,1)S(1)} %fusion.175), channel_id=1, source_target_pairs={{2,0},{4,2},{6,4},{8,6},{10,8},{12,10},{14,12},{16,14},{18,16},{20... | collective-permute-start | bytes 221192 | tf_op jit(solution)/shard_map/ppermute | solution.py:27
  664.6 16.0 %collective-permute-start.18 = (bf16[1,1,72,512]{3,2,1,0:T(8,128)(2,1)S(1)}, bf16[1,1,72,512]{3,2,1,0:T(8,128)(2,1)S(1)}, u32[]{:S(2)}, u32[]{:S(2)}) collective-permute-start(bf16[1,1,72,512]{3,2,1,0:T(8,128)(2,1)S(1)} %fusion.175), channel_id=1, source_target_pairs={{0,2},{2,4},{4,6},{6,8},{8,10},{10,12},{12,14},{14,16},{16,18},{18... | collective-permute-start | bytes 221192 | tf_op jit(solution)/shard_map/ppermute | solution.py:25
  688.9 395.0 %all-reduce.15.cloned.1.call-start = ((), (), s32[]{:S(2)}) async-start(), calls=%async_computation.17 | async-start | bytes 41943040 | tf_op jit(solution)/shard_map/psum | solution.py:281
  689.0 18.3 %copy-start.2 = (bf16[1,3,72,512]{3,2,1,0:T(8,128)(2,1)S(1)}, bf16[1,3,72,512]{3,2,1,0:T(8,128)(2,1)}, u32[]{:S(2)}) copy-start(bf16[1,3,72,512]{3,2,1,0:T(8,128)(2,1)} %copy-done.1) | copy-start | bytes 663556
  717.6 29.0 %copy-start.88 = (f32[256,2]{0,1:T(2,128)S(1)}, f32[256,2]{0,1:T(2,128)}, u32[]{:S(2)}) copy-start(f32[256,2]{0,1:T(2,128)} %param.43) | copy-start | bytes 6148
  717.6 29.0 %copy-start.93 = (f32[256,2]{0,1:T(2,128)S(1)}, f32[256,2]{0,1:T(2,128)}, u32[]{:S(2)}) copy-start(f32[256,2]{0,1:T(2,128)} %param.44) | copy-start | bytes 6148
  717.6 366.3 %copy-start.6 = (f32[3,3,64,512]{3,2,1,0:T(8,128)S(1)}, f32[3,3,64,512]{3,2,1,0:T(8,128)}, u32[]{:S(2)}) copy-start(f32[3,3,64,512]{3,2,1,0:T(8,128)} %param.34) | copy-start | bytes 3538948
  717.6 366.3 %copy-start.29 = (f32[3,3,64,512]{3,2,1,0:T(8,128)S(1)}, f32[3,3,64,512]{3,2,1,0:T(8,128)}, u32[]{:S(2)}) copy-start(f32[3,3,64,512]{3,2,1,0:T(8,128)} %param.35) | copy-start | bytes 3538948
  717.6 366.3 %copy-start.30 = (f32[3,3,64,512]{3,2,1,0:T(8,128)S(1)}, f32[3,3,64,512]{3,2,1,0:T(8,128)}, u32[]{:S(2)}) copy-start(f32[3,3,64,512]{3,2,1,0:T(8,128)} %param.36) | copy-start | bytes 3538948
  (85 other events, 635.4 us)
Sparse Core Ops, SparseCore 0:
  10.9 53.6 all-gather.5
  67.3 80.2 all-gather.7
  150.3 39.4 all-gather.9
  192.4 57.8 all-gather.11
  272.4 24.6 all-gather.13
  493.1 19.4 reduce-scatter.18
  537.0 10.9 reduce-scatter.10
  584.4 17.4 reduce-scatter.20
  635.3 11.6 reduce-scatter.12
  649.6 12.0 reduce-scatter.14
  689.0 12.7 reduce-scatter.16
  717.8 366.0 all-reduce.14
where the time goes:
time: 1120 us; the launch traced here: 1100 us
  waiting for transfers between devices  492 us (44%)
  local copies, waits for them, and re-layouts  229 us (20%)
  matrix products  114 us (10%)
  blocking collectives  100 us (9%)
  other arithmetic  85.3 us (8%)
  starting transfers between devices  60.9 us (5%)
  between operations  22.3 us (2%)
    psum x1, waiting for transfers between devices, body(): lax.psum(local_enter.astype(jnp.bfloat16), 'ha').astype(jnp.float32)  336 us
    unnamed x216, local copies, waits for them, and re-layouts  133 us
    dot_general x54, matrix products, tap_grads(): jnp.einsum('nhwc,nhwd->cd', window, upstream, preferred_element_type=jnp....  50.1 us
    all_gather x7, blocking collectives, gather_channels(): return lax.all_gather(values, 'col', axis=3, tiled=True)  49.6 us
    all_gather x1, waiting for transfers between devices, body(): lax.all_gather(w_middle.astype(jnp.bfloat16), 'ha', axis=2, tiled=True)  47.4 us
    conv_general_dilated x10, matrix products, convolve_rows(): lax.conv_general_dilated(padded, weight, (1, 1), ((0, 0), (1, 1)), dimens...  46.7 us
    another operation x18, local copies, waits for them, and re-layouts  46.2 us
    all_gather x1, waiting for transfers between devices, body(): lax.all_gather(w_upward.astype(jnp.bfloat16), 'ha', axis=2, tiled=True)  31.2 us
  transfers between devices with their start and end apart: 32, of which 8 were waited for; matrix products, arithmetic and copies ran while one was open for 31% of the time, Pallas kernels for 0%

commit v1 on v0

--- a/solution.py
+++ b/solution.py
@@ -1,6 +1,8 @@
 import jax
 import jax.numpy as jnp
 from jax import lax
+from jax.experimental import pallas as pl
+from jax.experimental.pallas import tpu as pltpu
 from jax.sharding import PartitionSpec as P
 
 STEP = 10
@@ -320,6 +322,856 @@
     )
 
 
+BF = jnp.bfloat16
+F32 = jnp.float32
+MESH = pl.DeviceIdType.MESH
+LANE = 128
+PI_PART = 0.7978845608028654
+CUBE = 0.044715
+
+
+def gelu_value(v):
+    return 0.5 * v * (1.0 + jnp.tanh(PI_PART * (v + CUBE * (v * v * v))))
+
+
+def gelu_slope(v):
+    bent = jnp.tanh(PI_PART * (v + CUBE * (v * v * v)))
+    inner = PI_PART * (1.0 + 3.0 * CUBE * (v * v))
+    return 0.5 * (1.0 + bent) + 0.5 * v * (1.0 - bent * bent) * inner
+
+
+def dot_nn(lhs, rhs):
+    return lax.dot_general(lhs, rhs, (((1,), (0,)), ((), ())), preferred_element_type=F32)
+
+
+def dot_nt(lhs, rhs):
+    return lax.dot_general(lhs, rhs, (((1,), (1,)), ((), ())), preferred_element_type=F32)
+
+
+def span(at, size):
+    return pl.ds(pl.multiple_of(at * size, size), size)
+
+
+SCRATCH = (
+    ("IN", (8, 2, 128, 128), BF),
+    ("SK", (4, 64, 512), BF),
+    ("LB", (16, 8, 128), F32),
+    ("W1", (9, 128, 128), BF),
+    ("W2", (9, 128, 256), BF),
+    ("WU", (16, 64, 256), BF),
+    ("W3", (9, 128, 512), BF),
+    ("W1T", (128, 1152), BF),
+    ("W2T", (256, 1152), BF),
+    ("WUT", (256, 1024), BF),
+    ("W3T", (512, 1152), BF),
+    ("X1", (1152, 2048), BF),
+    ("X2", (1152, 2048), BF),
+    ("X3", (1152, 2048), BF),
+    ("P1", (4, 32, 2048), F32),
+    ("P1b", (4, 32, 2048), BF),
+    ("R1", (3, 32, 2048), BF),
+    ("A1", (4, 32, 2048), BF),
+    ("P2b", (128, 2048), BF),
+    ("T2", (128, 2048), BF),
+    ("S2b", (4, 128, 512), BF),
+    ("R2", (3, 128, 512), BF),
+    ("pre2", (128, 512), F32),
+    ("A2", (8, 128, 512), BF),
+    ("J", (2, 4, 128, 768), BF),
+    ("P3b", (4, 64, 2048), BF),
+    ("T3", (4, 64, 2048), BF),
+    ("S3b", (4, 64, 2048), BF),
+    ("R3", (3, 64, 2048), BF),
+    ("pre3", (64, 2048), F32),
+    ("act3", (64, 2048), BF),
+    ("LG", (8, 32, 128), F32),
+    ("LBL", (32, 128), F32),
+    ("DL", (32, 128), F32),
+    ("G3", (8, 64, 2048), BF),
+    ("Z", (1152, 2048), F32),
+    ("HS", (2, 2, 64, 128), F32),
+    ("HR", (2, 2, 64, 128), F32),
+    ("DB", (4, 64, 128), F32),
+    ("DR", (256, 512), BF),
+    ("P8", (128, 2048), F32),
+    ("P7b", (4, 128, 512), BF),
+    ("T7", (4, 128, 512), BF),
+    ("S7b", (4, 128, 512), BF),
+    ("R7", (3, 128, 512), BF),
+    ("G2", (2, 128, 2048), BF),
+    ("P8b", (4, 32, 2048), BF),
+    ("R8", (3, 32, 2048), BF),
+    ("G1", (4, 32, 2048), BF),
+    ("GW3", (9, 128, 512), BF),
+    ("GWU", (16, 64, 256), BF),
+    ("GW2", (9, 128, 256), BF),
+    ("GW1", (9, 128, 128), BF),
+    ("RG3", (4, 9, 64, 256), BF),
+    ("RGU", (16, 64, 256), BF),
+    ("RG2", (9, 64, 512), BF),
+    ("RG1", (9, 32, 512), BF),
+    ("HD", (16, 8, 128), F32),
+)
+COPIES = 176
+
+
+def fused(widths, *refs):
+    wa, wb = widths
+    inT, skT, lab, head, w1, w2, wu, w3, g1o, g2o, guo, g3o, hdo = refs[:13]
+    m = {name: ref for (name, _, _), ref in zip(SCRATCH, refs[13:-2])}
+    send_sem, recv_sem = refs[-2:]
+    h, y = lax.axis_index("ha"), lax.axis_index("col")
+    z, x, e = lax.div(h, 4), lax.rem(lax.div(h, 2), 2), lax.rem(h, 2)
+    q = 2 * y + x
+    s = 2 * q + e
+    twin = h + 1 - 2 * e
+    started = []
+    count = [0]
+
+    def ha(z_, x_, e_):
+        return 4 * z_ + 2 * x_ + e_
+
+    def remote(src, dst, h2, y2, sem_s, sem_r):
+        return pltpu.make_async_remote_copy(
+            src_ref=src,
+            dst_ref=dst,
+            send_sem=send_sem.at[sem_s],
+            recv_sem=recv_sem.at[sem_r],
+            device_id={"ha": h2, "col": y2},
+            device_id_type=MESH,
+        )
+
+    def push(src, dst, h2, y2):
+        n = count[0]
+        count[0] += 1
+        copy = remote(src, dst, h2, y2, n, n)
+        copy.start()
+        started.append((copy, None))
+        return copy
+
+    def reserve(n):
+        base = count[0]
+        count[0] += n
+        return base
+
+    def hand(src, dst, h2, y2, sem_s, sem_r):
+        same = jnp.logical_and(h2 == h, y2 == y)
+        away = jnp.logical_not(same)
+        copy = remote(src, dst, h2, y2, sem_s, sem_r)
+
+        @pl.when(same)
+        def _():
+            pltpu.make_async_copy(src, dst, recv_sem.at[sem_r]).start()
+
+        @pl.when(away)
+        def _():
+            copy.start()
+
+        started.append((copy, away))
+
+    def landed(dst, sem_r):
+        remote(dst, dst, twin, y, sem_r, sem_r).wait_recv()
+
+    lanes = lax.broadcasted_iota(jnp.int32, (1, LANE), 1)
+    left_ok = jnp.logical_and(jnp.logical_and(lanes != 0, lanes != wa), lanes < wa + wb)
+    right_ok = jnp.logical_and(lanes != wa - 1, lanes < wa + wb - 1)
+
+    def from_left(v):
+        return jnp.where(left_ok, pltpu.roll(v, 1, 1), 0.0)
+
+    def from_right(v):
+        return jnp.where(right_ok, pltpu.roll(v, LANE - 1, 1), 0.0)
+
+    J, HR = m["J"], m["HR"]
+
+    @pl.when(z == 0)
+    def _():
+        J[1, 1:3, :, 0:128] = jnp.zeros((2, 128, 128), BF)
+        HR[0] = jnp.zeros((2, 64, 128), F32)
+
+    @pl.when(z == 3)
+    def _():
+        J[0, 1:3, :, 640:768] = jnp.zeros((2, 128, 128), BF)
+        HR[1] = jnp.zeros((2, 64, 128), F32)
+
+    IN, LB = m["IN"], m["LB"]
+    in_copies = []
+    for dz in range(4):
+        for dx in range(2):
+            if dz == 0 and dx == 0:
+                continue
+            zt = lax.rem(z + dz, 4)
+            xt = lax.rem(x + dx, 2)
+            in_copies.append(
+                push(inT.at[span(xt, 128)], IN.at[2 * z + x, e], ha(zt, xt, e), y)
+            )
+    IN[2 * z + x, e] = inT[span(x, 128), :]
+
+    W1, W2, WU, W3 = m["W1"], m["W2"], m["WU"], m["W3"]
+    b1 = reserve(4)
+    for i in range(4):
+        hand(
+            w1.at[:, :, i * 128 : i * 128 + 128],
+            W1.at[:, span(2 * x + e, 32), :],
+            ha(2 * y + i // 2, lax.rem(z, 2), i % 2),
+            lax.div(z, 2),
+            b1 + i,
+            b1 + 2 * x + e,
+        )
+    lab_copies = []
+    LB[h] = lab[...]
+    for d in range(1, 16):
+        lab_copies.append(push(lab, LB.at[h], lax.rem(h + d, 16), y))
+
+    for copy in in_copies:
+        copy.wait_recv()
+    twin_in = push(IN.at[:, e], IN.at[:, e], twin, y)
+
+    b2 = reserve(2)
+    for i in range(2):
+        hand(
+            w2.at[:, :, i * 256 : i * 256 + 256],
+            W2.at[:, span(e, 64), :],
+            ha(z, i, x),
+            y,
+            b2 + i,
+            b2 + e,
+        )
+    SK = m["SK"]
+    sk_copies = []
+    slot = 2 * x + e
+    for d in range(1, 4):
+        other = lax.rem(slot + d, 4)
+        sk_copies.append(push(skT.at[other], SK.at[slot], 4 * z + other, y))
+    SK[slot] = skT[slot]
+    bu_copies = []
+    for d in range(1, 16):
+        ht = lax.rem(h + d, 16)
+        bu_copies.append(push(wu.at[lax.rem(ht, 4)], WU.at[h], ht, y))
+    WU[h] = wu[slot]
+    b3 = reserve(4)
+    for i in range(4):
+        hand(
+            w3,
+            W3.at[:, span(lax.div(z, 2), 64), span(y, 256)],
+            ha(i, x, e),
+            lax.rem(z, 2),
+            b3 + i,
+            b3 + 2 * lax.div(z, 2) + y,
+        )
+
+    def patches(block, out):
+        def one(i, carry):
+            low = block(i)
+            v = low.astype(F32)
+            kinds = (from_left(v).astype(BF), low, from_right(v).astype(BF))
+            for di in (-1, 0, 1):
+                row = lax.rem(i - di + 16, 16)
+                for dj in range(3):
+                    tap = (di + 1) * 3 + dj
+                    out[tap * 128 : tap * 128 + 128, span(row, 128)] = kinds[dj]
+            return carry
+
+        lax.fori_loop(0, 16, one, 0)
+        zero = jnp.zeros((384, 128), BF)
+        out[0:384, 0:128] = zero
+        out[768:1152, 1920:2048] = zero
+
+    def transposed(weight, out, rows):
+        for t in range(weight.shape[0]):
+            out[:, t * rows : t * rows + rows] = weight[t].T
+
+    for j in range(4):
+        landed(W1.at[:, 32 * j : 32 * j + 32, :], b1 + j)
+    transposed(W1, m["W1T"], 128)
+    twin_in.wait_recv()
+    X1, X2, X3 = m["X1"], m["X2"], m["X3"]
+    patches(lambda i: IN[lax.div(i, 2), lax.rem(i, 2)], X1)
+    P1, P1b, R1, A1 = m["P1"], m["P1b"], m["R1"], m["A1"]
+
+    def conv_one(n, carry):
+        cols = span(n, 512)
+        total = dot_nn(m["W1T"][...], X1[:, cols]).reshape(4, 32, 512)
+        P1[:, :, cols] = total
+        P1b[:, :, cols] = total.astype(BF)
+        return carry
+
+    lax.fori_loop(0, 4, conv_one, 0)
+
+    def to_plane(d):
+        there = lax.rem(q + d, 4)
+        return there, ha(z, lax.rem(there, 2), e), lax.div(there, 2)
+
+    def scatter(source, slots):
+        copies = []
+        for d in range(1, 4):
+            there, h2, y2 = to_plane(d)
+            copies.append(push(source.at[there], slots.at[d - 1], h2, y2))
+        return copies
+
+    def gather_four(buf):
+        copies = []
+        for d in range(1, 4):
+            _, h2, y2 = to_plane(d)
+            copies.append(push(buf.at[q], buf.at[q], h2, y2))
+        return copies
+
+    def gather_plane(buf):
+        copies = []
+        for d in range(1, 4):
+            _, h2, y2 = to_plane(d)
+            copies.append(push(buf.at[s], buf.at[s], h2, y2))
+        last = [push(buf.at[s], buf.at[s], twin, y)]
+        for d in range(1, 4):
+            copies[d - 1].wait_recv()
+            came = 2 * lax.rem(q + 4 - d, 4) + e
+            last.append(push(buf.at[came], buf.at[came], twin, y))
+        return last
+
+    def arrive(copies):
+        for copy in copies:
+            copy.wait_recv()
+
+    arrive(scatter(P1b, R1))
+
+    def act_one(n, carry):
+        cols = span(n, 512)
+        total = P1[q, :, cols] + R1[0, :, cols].astype(F32)
+        total = total + R1[1, :, cols].astype(F32) + R1[2, :, cols].astype(F32)
+        P1[q, :, cols] = total
+        A1[q, :, cols] = gelu_value(total).astype(BF)
+        return carry
+
+    lax.fori_loop(0, 4, act_one, 0)
+    wait_one = gather_four(A1)
+    for j in range(2):
+        landed(W2.at[:, 64 * j : 64 * j + 64, :], b2 + j)
+    transposed(W2, m["W2T"], 128)
+    arrive(wait_one)
+
+    patches(lambda i: A1[:, :, span(i, 128)].reshape(128, 128), X2)
+    Z, P2b, T2, S2b, R2 = m["Z"], m["P2b"], m["T2"], m["S2b"], m["R2"]
+
+    def conv_two(n, carry):
+        cols = span(n, 512)
+        Z[0:256, cols] = dot_nn(m["W2T"][...], X2[:, cols])
+        P2b[:, cols] = Z[span(1 - e, 128), cols].astype(BF)
+        return carry
+
+    lax.fori_loop(0, 4, conv_two, 0)
+    arrive([push(P2b, T2, twin, y)])
+
+    def pair_two(n, carry):
+        cols = span(n, 512)
+        total = Z[span(e, 128), cols] + T2[:, cols].astype(F32)
+        Z[span(e, 128), cols] = total
+        S2b[n] = total.astype(BF)
+        return carry
+
+    lax.fori_loop(0, 4, pair_two, 0)
+    two = []
+    for d in range(1, 4):
+        zt = lax.rem(z + d, 4)
+        two.append(push(S2b.at[zt], R2.at[d - 1], ha(zt, x, e), y))
+    for d in range(1, 16):
+        bu_copies[d - 1].wait_recv()
+    for t in range(8):
+        m["WUT"][:, t * 128 : t * 128 + 128] = WU[2 * t : 2 * t + 2].reshape(128, 256).T
+    arrive(two)
+    pre2, A2 = m["pre2"], m["A2"]
+    total = Z[span(e, 128), span(z, 512)] + R2[0].astype(F32)
+    total = total + R2[1].astype(F32) + R2[2].astype(F32)
+    pre2[...] = total
+    A2[s] = gelu_value(total).astype(BF)
+    wait_two = gather_plane(A2)
+    for copy in sk_copies:
+        copy.wait_recv()
+    for a in range(2):
+        for b in range(2):
+            p = 2 * a + b
+            for i in range(4):
+                J[a, 1 + b, 64:128, 128 + 128 * i : 256 + 128 * i] = SK[i, :, p * 128 : p * 128 + 128]
+    arrive(wait_two)
+
+    for p in range(4):
+        plane = dot_nn(m["WUT"][p * 64 : p * 64 + 64, :], A2[...].reshape(1024, 512))
+        J[p // 2, 1 + p % 2, 0:64, 128:640] = plane.astype(BF)
+
+    def fringe(part, up, down, send_down, keep_down, send_up, keep_up):
+        below = remote(send_down, keep_down, lax.rem(h + 4, 16), y, down, down)
+        above = remote(send_up, keep_up, lax.rem(h + 12, 16), y, up, up)
+
+        @pl.when(z < 3)
+        def _():
+            below.start()
+
+        @pl.when(z > 0)
+        def _():
+            above.start()
+
+        started.append((below, z < 3))
+        started.append((above, z > 0))
+
+        def wait():
+            @pl.when(z > 0)
+            def _():
+                below.wait_recv()
+
+            @pl.when(z < 3)
+            def _():
+                above.wait_recv()
+
+        return wait
+
+    bj = reserve(2)
+    fringe(
+        None,
+        bj,
+        bj + 1,
+        J.at[1, 1:3, :, 512:640],
+        J.at[1, 1:3, :, 0:128],
+        J.at[0, 1:3, :, 128:256],
+        J.at[0, 1:3, :, 640:768],
+    )()
+    for a in range(2):
+        for i in range(1 - a, 6 - a):
+            at = slice(i * 128, i * 128 + 128)
+            J[a, 0, :, at] = from_left(J[a, 2, :, at].astype(F32)).astype(BF)
+            J[a, 3, :, at] = from_right(J[a, 1, :, at].astype(F32)).astype(BF)
+    for a in range(2):
+        for b in range(2):
+            p = 2 * a + b
+            for da in range(3):
+                up, di = (a + da - 1) % 2, (a + da - 1) // 2
+                for db in range(3):
+                    tap = da * 3 + db
+                    X3[tap * 128 : tap * 128 + 128, p * 512 : p * 512 + 512] = J[
+                        up, b + db, :, (1 + di) * 128 : (5 + di) * 128
+                    ]
+
+    for j in range(4):
+        t, half = j // 2, j % 2
+        landed(W3.at[:, 64 * t : 64 * t + 64, 256 * half : 256 * half + 256], b3 + j)
+    transposed(W3, m["W3T"], 128)
+    P3b, T3, S3b, R3 = m["P3b"], m["T3"], m["S3b"], m["R3"]
+
+    def conv_three(n, carry):
+        cols = span(n, 256)
+        Z[0:512, cols] = dot_nn(m["W3T"][...], X3[:, cols])
+        for k in range(4):
+            P3b[k, :, cols] = Z[span(2 * k + 1 - e, 64), cols].astype(BF)
+        return carry
+
+    lax.fori_loop(0, 8, conv_three, 0)
+    arrive([push(P3b, T3, twin, y)])
+
+    def pair_three(n, carry):
+        cols = span(n, 512)
+        for k in range(4):
+            total = Z[span(2 * k + e, 64), cols] + T3[k, :, cols].astype(F32)
+            Z[span(2 * k + e, 64), cols] = total
+            S3b[k, :, cols] = total.astype(BF)
+        return carry
+
+    lax.fori_loop(0, 4, pair_three, 0)
+    arrive(scatter(S3b, R3))
+    pre3, act3, LG = m["pre3"], m["act3"], m["LG"]
+    wide = (64, LANE)
+    h0 = jnp.broadcast_to(head[:, 0:1], wide)
+    h1 = jnp.broadcast_to(head[:, 1:2], wide)
+    for b in range(16):
+        cols = slice(b * 128, b * 128 + 128)
+        total = Z[span(s, 64), cols] + R3[0, :, cols].astype(F32)
+        total = total + R3[1, :, cols].astype(F32) + R3[2, :, cols].astype(F32)
+        pre3[:, cols] = total
+        act = gelu_value(total).astype(BF)
+        act3[:, cols] = act
+        act = act.astype(F32)
+        LG[s, b : b + 1, :] = jnp.sum(act * h0, axis=0, keepdims=True)
+        LG[s, 16 + b : 17 + b, :] = jnp.sum(act * h1, axis=0, keepdims=True)
+    wait_logits = gather_plane(LG)
+    for copy in lab_copies:
+        copy.wait_recv()
+    LBL = m["LBL"]
+    for p in range(4):
+        for i in range(4):
+            LBL[p * 4 + i : p * 4 + i + 1, :] = LB[4 * z + i, p : p + 1, :]
+            LBL[16 + p * 4 + i : 17 + p * 4 + i, :] = LB[4 * z + i, 4 + p : 5 + p, :]
+    every = jnp.sum(LB[...], axis=0)
+    labelled = jnp.sum(jnp.sum(every[4:8, :], axis=0, keepdims=True), axis=1, keepdims=True)
+    arrive(wait_logits)
+
+    logits = LG[0]
+    for k in range(1, 8):
+        logits = logits + LG[k]
+    zero, one = logits[0:16, :], logits[16:32, :]
+    picks, usable = LBL[0:16, :] > 0.5, LBL[16:32, :]
+    top = jnp.maximum(zero, one)
+    lse = top + jnp.log(jnp.exp(zero - top) + jnp.exp(one - top))
+    logp = jnp.where(picks, one, zero) - lse
+    rest = jnp.exp(jnp.where(picks, zero, one) - lse)
+    chance = jnp.exp(logp)
+    gap = 1.0 - chance
+    terms = usable * (-(gap * gap) * logp)
+    slope = (2.0 * gap * chance * logp - gap * gap) * usable / labelled
+    own, other = slope * gap, -slope * rest
+    DL = m["DL"]
+    DL[0:16, :] = jnp.where(picks, other, own).astype(BF).astype(F32)
+    DL[16:32, :] = jnp.where(picks, own, other).astype(BF).astype(F32)
+    loss = jnp.sum(jnp.sum(terms, axis=0, keepdims=True), axis=1, keepdims=True)
+    G3, HD = m["G3"], m["HD"]
+    sum0 = jnp.zeros(wide, F32)
+    sum1 = jnp.zeros(wide, F32)
+    for b in range(16):
+        cols = slice(b * 128, b * 128 + 128)
+        d0 = jnp.broadcast_to(DL[b : b + 1, :], wide)
+        d1 = jnp.broadcast_to(DL[16 + b : 17 + b, :], wide)
+        G3[s, :, cols] = ((h0 * d0 + h1 * d1) * gelu_slope(pre3[:, cols])).astype(BF)
+        act = act3[:, cols].astype(F32)
+        sum0 = sum0 + act * d0
+        sum1 = sum1 + act * d1
+    wait_g3 = gather_plane(G3)
+    side = lax.broadcasted_iota(jnp.int32, wide, 1)
+    sum0 = jnp.sum(sum0, axis=1, keepdims=True)
+    sum1 = jnp.sum(sum1, axis=1, keepdims=True)
+    tile = jnp.where(side == 0, sum0, jnp.where(side == 1, sum1, 0.0))
+    HD[h, 0:8, 0:64] = tile.T[0:8, :]
+    HD[h, 2:3, 0:64] = jnp.broadcast_to(loss, (1, 64))
+    hd_copies = []
+    for d in range(1, 16):
+        hd_copies.append(push(HD.at[h], HD.at[h], lax.rem(h + d, 16), y))
+    arrive(wait_g3)
+
+    HS, DB, DR = m["HS"], m["DB"], m["DR"]
+
+    def back_three(n, carry):
+        cols = span(n, 256)
+        Z[0:576, cols] = dot_nn(
+            W3[:, 0:64, :].reshape(576, 512), G3[:, :, cols].reshape(512, 256)
+        )
+        return carry
+
+    lax.fori_loop(0, 8, back_three, 0)
+    ways = (((0, 0, 0), (1, -1, 0), (1, 1, 1)), ((0, -1, -1), (0, 1, 0), (1, 0, 0)))
+
+    def raised_block(a, b, i):
+        straight, bent = [], []
+        for ao, da, di in ways[a]:
+            io = i - di
+            if io < 0 or io > 3 or (i < 0 or i > 3) and di == 0:
+                continue
+            for bo, db, dj in ways[b]:
+                tap = (da + 1) * 3 + db + 1
+                at = ((2 * ao + bo) * 4 + io) * 128
+                (straight if dj == 0 else bent).append(Z[tap * 64 : tap * 64 + 64, at : at + 128])
+        turned = sum(bent[1:], bent[0])
+        turned = from_left(turned) if b == 0 else from_right(turned)
+        return sum(straight, turned)
+
+    for b in range(2):
+        HS[0, b] = raised_block(0, b, 4)
+        HS[1, b] = raised_block(1, b, -1)
+    bh = reserve(2)
+    wait_fringe = fringe(None, bh, bh + 1, HS.at[0], HR.at[0], HS.at[1], HR.at[1])
+    for a in range(2):
+        for b in range(2):
+            p = 2 * a + b
+            for i in range(4):
+                block = raised_block(a, b, i)
+                if i == 3 * a:
+                    DB[p] = block
+                else:
+                    DR[p * 64 : p * 64 + 64, i * 128 : i * 128 + 128] = block.astype(BF)
+    wait_fringe()
+    for a in range(2):
+        for b in range(2):
+            p = 2 * a + b
+            DR[p * 64 : p * 64 + 64, a * 384 : a * 384 + 128] = (DB[p] + HR[a, b]).astype(BF)
+
+    P7b, T7, S7b, R7 = m["P7b"], m["T7"], m["S7b"], m["R7"]
+
+    def back_up(k, carry):
+        Z[span(k, 128), 0:512] = dot_nn(WU[pl.ds(2 * k, 2)].reshape(128, 256), DR[...])
+        return carry
+
+    lax.fori_loop(0, 8, back_up, 0)
+    for k in range(4):
+        P7b[k] = Z[span(2 * k + 1 - e, 128), 0:512].astype(BF)
+    wait_pair = push(P7b, T7, twin, y)
+
+    GW3, GWU, GW2, GW1 = m["GW3"], m["GWU"], m["GW2"], m["GW1"]
+    RG3, RGU, RG2, RG1 = m["RG3"], m["RGU"], m["RG2"], m["RG1"]
+
+    def pair_seven():
+        for k in range(4):
+            total = Z[span(2 * k + e, 128), 0:512] + T7[k].astype(F32)
+            Z[span(2 * k + e, 128), 0:512] = total
+            S7b[k] = total.astype(BF)
+
+    wait_pair.wait_recv()
+    pair_seven()
+    wait_seven = scatter(S7b, R7)
+
+    def grad_three(t, carry):
+        GW3[t] = dot_nt(X3[span(t, 128), :], G3[...].reshape(512, 2048)).astype(BF)
+        return carry
+
+    lax.fori_loop(0, 9, grad_three, 0)
+
+    def grad_up(k, carry):
+        GWU[pl.ds(2 * k, 2)] = dot_nt(A2[k], DR[...]).astype(BF).reshape(2, 64, 256)
+        return carry
+
+    lax.fori_loop(0, 8, grad_up, 0)
+    arrive(wait_seven)
+    G2 = m["G2"]
+    total = Z[span(s, 128), 0:512] + R7[0].astype(F32)
+    total = total + R7[1].astype(F32) + R7[2].astype(F32)
+    G2[e, :, span(z, 512)] = (total * gelu_slope(pre2[...])).astype(BF)
+    mine = G2.at[e, :, span(z, 512)]
+    g2_copies = []
+    for d in range(1, 4):
+        zt = lax.rem(z + d, 4)
+        g2_copies.append(push(mine, mine, ha(zt, x, e), y))
+    g2_last = [push(mine, mine, twin, y)]
+    for d in range(1, 4):
+        g2_copies[d - 1].wait_recv()
+        came = G2.at[e, :, span(lax.rem(z + 4 - d, 4), 512)]
+        g2_last.append(push(came, came, twin, y))
+
+    bg3 = reserve(4)
+    for j in range(4):
+        t, half = j // 2, j % 2
+        hand(
+            GW3.at[:, 64 * t : 64 * t + 64, 256 * half : 256 * half + 256],
+            RG3.at[z],
+            ha(2 * t + y, x, e),
+            half,
+            bg3 + j,
+            bg3 + z,
+        )
+    gu_copies = []
+    for d in range(1, 16):
+        ht = lax.rem(h + d, 16)
+        gu_copies.append(push(GWU.at[ht], RGU.at[h], ht, y))
+    RGU[h] = GWU[h]
+    arrive(g2_last)
+
+    def back_two(n, carry):
+        cols = span(n, 256)
+        Z[:, cols] = dot_nn(W2[...].reshape(1152, 256), G2[:, :, cols].reshape(256, 256))
+        return carry
+
+    lax.fori_loop(0, 8, back_two, 0)
+    P8b, R8, G1 = m["P8b"], m["R8"], m["G1"]
+    P8 = m["P8"]
+
+    def fold(i, carry):
+        sums = []
+        for dj in range(3):
+            part = None
+            for di in range(3):
+                row = i - (di - 1)
+                inside = jnp.logical_and(row >= 0, row <= 15)
+                row = jnp.clip(row, 0, 15)
+                tap = di * 3 + dj
+                block = jnp.where(inside, Z[tap * 128 : tap * 128 + 128, span(row, 128)], 0.0)
+                part = block if part is None else part + block
+            sums.append(part)
+        total = sums[1] + from_right(sums[0]) + from_left(sums[2])
+        P8[:, span(i, 128)] = total
+        P8b[:, :, span(i, 128)] = total.reshape(4, 32, 128).astype(BF)
+        return carry
+
+    lax.fori_loop(0, 16, fold, 0)
+    wait_eight = scatter(P8b, R8)
+
+    def grad_two(t, carry):
+        GW2[t] = dot_nt(X2[span(t, 128), :], G2[...].reshape(256, 2048)).astype(BF)
+        return carry
+
+    lax.fori_loop(0, 9, grad_two, 0)
+    arrive(wait_eight)
+
+    def act_back(n, carry):
+        cols = span(n, 512)
+        total = P8[span(q, 32), cols] + R8[0, :, cols].astype(F32)
+        total = total + R8[1, :, cols].astype(F32) + R8[2, :, cols].astype(F32)
+        G1[q, :, cols] = (total * gelu_slope(P1[q, :, cols])).astype(BF)
+        return carry
+
+    lax.fori_loop(0, 4, act_back, 0)
+    wait_g1 = gather_four(G1)
+    bg2 = reserve(2)
+    for j in range(2):
+        hand(
+            GW2.at[:, 64 * j : 64 * j + 64, :],
+            RG2.at[:, :, span(x, 256)],
+            ha(z, e, j),
+            y,
+            bg2 + j,
+            bg2 + x,
+        )
+    arrive(wait_g1)
+
+    def grad_one(t, carry):
+        GW1[t] = dot_nt(X1[span(t, 128), :], G1[...].reshape(128, 2048)).astype(BF)
+        return carry
+
+    lax.fori_loop(0, 9, grad_one, 0)
+    bg1 = reserve(4)
+    r_low = 2 * lax.rem(z, 2) + e
+    for j in range(4):
+        hand(
+            GW1.at[:, 32 * j : 32 * j + 32, :],
+            RG1.at[:, :, span(r_low, 128)],
+            ha(q, j // 2, j % 2),
+            lax.div(z, 2),
+            bg1 + j,
+            bg1 + r_low,
+        )
+
+    for copy in hd_copies:
+        copy.wait_recv()
+    for j in range(4):
+        hdo[j] = HD[j] + HD[4 + j] + HD[8 + j] + HD[12 + j]
+    hdo[4] = jnp.broadcast_to(labelled, (8, 128))
+    for k in range(4):
+        landed(RG3.at[k], bg3 + k)
+    for t in range(9):
+        g3o[t] = (RG3[0, t].astype(F32) + RG3[1, t].astype(F32)) + (
+            RG3[2, t].astype(F32) + RG3[3, t].astype(F32)
+        )
+    for copy in gu_copies:
+        copy.wait_recv()
+    for k in range(4):
+        guo[k] = (RGU[k].astype(F32) + RGU[4 + k].astype(F32)) + (
+            RGU[8 + k].astype(F32) + RGU[12 + k].astype(F32)
+        )
+    for k in range(2):
+        landed(RG2.at[:, :, 256 * k : 256 * k + 256], bg2 + k)
+    g2o[...] = RG2[...]
+    for k in range(4):
+        landed(RG1.at[:, :, 128 * k : 128 * k + 128], bg1 + k)
+    g1o[...] = RG1[...]
+    for copy, when in started:
+        if when is None:
+            copy.wait_send()
+        else:
+            pl.when(when)(copy.wait_send)
+
+
+def parity_planes(rows):
+    _, two, across, chans = rows.shape
+    split = rows.reshape(two, across // 2, 2, chans)
+    return split.transpose(3, 0, 2, 1)
+
+
+def lane_blocks(first, second):
+    free = LANE - first.shape[-1] - second.shape[-1]
+    both = jnp.concatenate([first, second], axis=-1)
+    return jnp.pad(both, [(0, 0)] * (both.ndim - 1) + [(0, free)])
+
+
+def resident_body(
+    input_a,
+    input_b,
+    skip_a,
+    skip_b,
+    labels_a,
+    labels_b,
+    valid_a,
+    valid_b,
+    w_enter,
+    moment_enter,
+    square_enter,
+    w_middle,
+    moment_middle,
+    square_middle,
+    w_upward,
+    moment_upward,
+    square_upward,
+    w_merge,
+    moment_merge,
+    square_merge,
+    w_head,
+    moment_head,
+    square_head,
+):
+    slot = lax.rem(lax.axis_index("ha"), 4)
+    pixels = lane_blocks(input_a[0, 0].T, input_b[0, 0].T)
+    skips = lane_blocks(parity_planes(skip_a), parity_planes(skip_b)).reshape(4, 64, 512)
+    marks = jnp.concatenate(
+        [
+            lane_blocks(parity_planes(one[..., None]), parity_planes(two[..., None])).reshape(4, LANE)
+            for one, two in ((labels_a, labels_b), (valid_a, valid_b))
+        ]
+    ).astype(F32)
+    head_low = w_head.astype(BF).astype(F32)
+    head_own = jnp.pad(lax.dynamic_slice_in_dim(head_low, slot * 64, 64, 0), ((0, 0), (0, 126)))
+    upward = w_upward.astype(BF).reshape(4, 64, 4, 64).transpose(2, 1, 0, 3).reshape(4, 64, 256)
+    vmem = pl.BlockSpec(memory_space=pltpu.VMEM)
+    g1, g2, gu, g3, hd = pl.pallas_call(
+        lambda *refs: fused((input_a.shape[2], input_b.shape[2]), *refs),
+        out_shape=(
+            jax.ShapeDtypeStruct((9, 32, 512), BF),
+            jax.ShapeDtypeStruct((9, 64, 512), BF),
+            jax.ShapeDtypeStruct((4, 64, 256), F32),
+            jax.ShapeDtypeStruct((9, 64, 256), F32),
+            jax.ShapeDtypeStruct((5, 8, 128), F32),
+        ),
+        in_specs=[vmem] * 8,
+        out_specs=[vmem] * 5,
+        scratch_shapes=[pltpu.VMEM(shape, kind) for _, shape, kind in SCRATCH]
+        + [pltpu.SemaphoreType.DMA((COPIES,)), pltpu.SemaphoreType.DMA((COPIES,))],
+        compiler_params=pltpu.CompilerParams(
+            has_side_effects=True, vmem_limit_bytes=60 * 1024 * 1024
+        ),
+    )(
+        pixels,
+        skips,
+        marks,
+        head_own,
+        w_enter.astype(BF).reshape(9, 32, 512),
+        w_middle.astype(BF).reshape(9, 64, 512),
+        upward,
+        w_merge.astype(BF).reshape(9, 64, 256),
+    )
+    grad_enter = g1.astype(F32).reshape(w_enter.shape)
+    grad_middle = g2.astype(F32).reshape(w_middle.shape)
+    grad_upward = gu.reshape(4, 64, 4, 64).transpose(2, 1, 0, 3).reshape(w_upward.shape)
+    grad_merge = g3.reshape(w_merge.shape)
+    grad_head = hd[0:4, 0:2, 0:64].transpose(0, 2, 1).reshape(w_head.shape)
+    return (
+        *adamw(w_enter, moment_enter, square_enter, grad_enter),
+        *adamw(w_middle, moment_middle, square_middle, grad_middle),
+        *adamw(w_upward, moment_upward, square_upward, grad_upward),
+        *adamw(w_merge, moment_merge, square_merge, grad_merge),
+        *adamw(w_head, moment_head, square_head, grad_head),
+        hd[0, 2, 0],
+        hd[4, 0, 0],
+    )
+
+
+def chosen(*args):
+    input_a, input_b, skip_a = args[0], args[1], args[2]
+    w_enter, w_middle, w_upward, w_merge = args[8], args[11], args[14], args[17]
+    fits = (
+        lax.axis_size("ha") == 16
+        and lax.axis_size("col") == 2
+        and input_a.shape[:2] == (1, 1)
+        and input_b.shape[:2] == (1, 1)
+        and input_a.shape[3] == 256
+        and skip_a.shape[3] == 256
+        and input_a.shape[2] + input_b.shape[2] <= LANE
+        and w_enter.shape == (3, 3, 32, 512)
+        and w_middle.shape == (3, 3, 64, 512)
+        and w_upward.shape == (2, 2, 64, 256)
+        and w_merge.shape == (3, 3, 64, 256)
+    )
+    return resident_body(*args) if fits else body(*args)
+
+
 def solution(mesh):
     placed = (
         P(None, "ha", None, "col"),
@@ -347,7 +1199,7 @@
         P("col", None),
     )
     return jax.shard_map(
-        body,
+        chosen,
         mesh=mesh,
         in_specs=placed,
         out_specs=(

time: 1120 us -> 276 us (0.25)
  the two profiles are of different devices: /device:TPU:14 before, /device:TPU:3 now
where the time goes in v1:
time: 276 us; the launch traced here: 275 us
  Pallas kernels  241 us (87%)
  local copies, waits for them, and re-layouts  17.1 us (6%)
  other arithmetic  16 us (6%)
    pallas_call x1, Pallas kernels, resident_body(): pl.pallas_call(lambda *refs: fused((input_a.shape[2], input_b.shape[2]),...  241 us
    convert_element_type x5, other arithmetic, adamw(): return (master_new, moment_new, square_new, master_new.astype(jnp.bfloat16))  9.67 us

profile of v1, /device:TPU:3, one launch (start us, length us, event | category | flops | bytes accessed | tf_op | source)
XLA Modules:
  0.0 275.4 jit_solution(15372703732823046500)
XLA Ops:
  0.7 0.8 fusion.13
  1.4 0.1 copy.78
  1.5 0.6 pad.23.refs_3_
  2.1 1.0 reshape.99
  3.1 0.0 copy-start.4
  3.1 0.4 copy.69
  3.5 0.9 reshape.98
  4.5 0.2 copy.68
  4.7 0.8 fusion.8
  5.5 0.0 copy-start
  5.5 0.8 reshape.100.refs_1_
  6.4 0.2 reshape.105
  6.5 0.2 copy.80
  6.8 0.9 reshape.106.refs_6_
  7.6 0.9 convert_element_type.48
  8.5 0.8 convert_element_type.47
  9.3 0.7 convert_element_type.50
  10.1 0.1 reshape_broadcast_in_dim.15
  10.2 0.1 copy.73
  10.3 0.1 reshape_broadcast_in_dim.14
  10.4 0.1 copy.72
  10.5 0.1 pad_add_fusion.1
  10.6 0.0 copy-done.16
  10.6 0.8 reshape_broadcast_in_dim.13
  11.4 1.1 copy.71
  12.4 0.8 reshape_broadcast_in_dim.12
  13.2 0.9 copy.70
  14.1 0.1 pad_add_fusion
  14.2 0.6 add_convert_fusion.refs_2_
  14.8 1.5 copy.66
  16.2 1.5 copy.67
  17.7 1.6 fusion.11.refs_0_
  19.3 241.4 %shard_map.390 = (bf16[9,32,512]{2,1,0:T(8,128)(2,1)}, bf16[9,64,512]{2,1,0:T(8,128)(2,1)}, f32[4,64,256]{2,1,0:T(8,128)}, f32[9,64,256]{2,1,0:T(8,128)}, f32[5,8,128]{2,1,0:T(8,128)}) custom-call(bf16[256,128]{1,0:T(8,128)(2,1)} %fusion.11.refs_0_, bf16[4,64,512]{2,1,0:T(8,128)(2,1)} %reshape.100.refs_1_, f32[8,128]{1,0:T(8,128)} %add_convert_fusion.refs_2_, ...), custom_call_target="tpu_custom_call" | custom-call | tf_op jit(solution)/shard_map/pallas_call | solution.py:1114
  260.7 0.7 slice_bitcast_fusion
  261.5 0.1 reshape.115
  261.5 1.3 fusion.14
  262.9 4.1 %fusion.20 = (bf16[3,3,64,512]{3,2,1,0:T(8,128)(2,1)}, f32[3,3,64,512]{3,2,1,0:T(8,128)}, f32[3,3,64,512]{3,2,1,0:T(8,128)}, f32[3,3,64,512]{3,2,1,0:T(8,128)}) fusion(f32[3,3,64,512]{3,2,1,0:T(8,128)S(1)} %copy-done, bf16[3,3,64,512]{3,2,1,0:T(8,128)(2,1)} %bitcast.46, f32[3,3,64,512]{3,2,1,0:T(8,128)S(1)} %copy-done.3, f32[3,3,64,512]{3,2,1,0:T(8,128)} %param.36), kind=kLoop, calls=%fused_computation.42 | loop fusion | flops 5013504 | bytes 8257536 | tf_op jit(solution)/shard_map/convert_element_type | solution.py:212
  267.0 1.2 reshape.112
  268.2 0.3 copy.76
  268.6 0.3 reshape.113
  269.0 1.0 fusion.18
  270.0 0.1 copy-done.6
  270.1 0.4 copy-done.7
  270.5 0.2 copy-done.8
  270.7 1.6 fusion.16
  272.3 0.3 copy-done.11
  272.6 1.6 fusion.23
  274.2 1.2 fusion.26
  (35 shorter events, 0.1 us)
Async XLA Ops:
  3.1 3.2 %copy-start.4 = (f32[2,2,64,256]{3,2,1,0:T(8,128)S(1)}, f32[2,2,64,256]{3,2,1,0:T(8,128)}, u32[]{:S(2)}) copy-start(f32[2,2,64,256]{3,2,1,0:T(8,128)} %param.37) | copy-start | bytes 786436
  5.5 2.1 copy-start
  6.7 1.8 copy-start.2
  7.6 1.7 copy-start.1
  8.5 1.5 copy-start.15
  8.5 1.7 copy-start.17
  8.5 2.1 copy-start.16
  8.5 3.9 %copy-start.18 = (s32[1,2,96]{2,1,0:T(2,128)S(1)}, s32[1,2,96]{2,1,0:T(2,128)}, u32[]{:S(2)}) copy-start(s32[1,2,96]{2,1,0:T(2,128)} %param.27) | copy-start | bytes 2308
  10.6 251.0 %copy-start.14 = (f32[256,2]{0,1:T(2,128)S(1)}, f32[256,2]{0,1:T(2,128)}, u32[]{:S(2)}) copy-start(f32[256,2]{0,1:T(2,128)} %param.43) | copy-start | bytes 6148
  11.4 251.5 %copy-start.3 = (f32[3,3,64,512]{3,2,1,0:T(8,128)S(1)}, f32[3,3,64,512]{3,2,1,0:T(8,128)}, u32[]{:S(2)}) copy-start(f32[3,3,64,512]{3,2,1,0:T(8,128)} %param.35) | copy-start | bytes 3538948
  267.0 2.0 copy-start.5
  267.0 2.0 copy-start.12
  267.0 2.0 copy-start.13
  268.9 1.2 copy-start.6
  268.9 1.6 copy-start.7
  269.0 1.7 copy-start.8
  270.7 1.6 copy-start.9
  270.7 1.6 copy-start.10
  270.7 1.9 copy-start.11

commit v2 on v1

--- a/solution.py
+++ b/solution.py
@@ -353,7 +353,15 @@
 
 
 SCRATCH = (
-    ("IN", (8, 2, 128, 128), BF),
+    ("inT", (2, 4, 32, 128), BF),
+    ("skT", (4, 64, 512), BF),
+    ("lab", (8, 128), F32),
+    ("flat", (4, 256, 128), F32),
+    ("w1", (9, 32, 512), BF),
+    ("w2", (9, 64, 512), BF),
+    ("wu", (4, 64, 256), BF),
+    ("w3", (9, 64, 256), BF),
+    ("IN", (8, 2, 4, 32, 128), BF),
     ("SK", (4, 64, 512), BF),
     ("LB", (16, 8, 128), F32),
     ("W1", (9, 128, 128), BF),
@@ -364,9 +372,7 @@
     ("W2T", (256, 1152), BF),
     ("WUT", (256, 1024), BF),
     ("W3T", (512, 1152), BF),
-    ("X1", (1152, 2048), BF),
-    ("X2", (1152, 2048), BF),
-    ("X3", (1152, 2048), BF),
+    ("X", (1152, 2048), BF),
     ("P1", (4, 32, 2048), F32),
     ("P1b", (4, 32, 2048), BF),
     ("R1", (3, 32, 2048), BF),
@@ -417,8 +423,9 @@
 
 def fused(widths, *refs):
     wa, wb = widths
-    inT, skT, lab, head, w1, w2, wu, w3, g1o, g2o, guo, g3o, hdo = refs[:13]
-    m = {name: ref for (name, _, _), ref in zip(SCRATCH, refs[13:-2])}
+    rows_a, rows_b, skip_a, skip_b, marks_a, marks_b, f1, f2, fu, f3, fh = refs[:11]
+    g1o, g2o, guo, g3o, hdo = refs[11:16]
+    m = {name: ref for (name, _, _), ref in zip(SCRATCH, refs[16:-2])}
     send_sem, recv_sem = refs[-2:]
     h, y = lax.axis_index("ha"), lax.axis_index("col")
     z, x, e = lax.div(h, 4), lax.rem(lax.div(h, 2), 2), lax.rem(h, 2)
@@ -494,29 +501,63 @@
         J[0, 1:3, :, 640:768] = jnp.zeros((2, 128, 128), BF)
         HR[1] = jnp.zeros((2, 64, 128), F32)
 
+    inT, skT, lab, flat = m["inT"], m["skT"], m["lab"], m["flat"]
+    w1, w2, wu, w3 = m["w1"], m["w2"], m["wu"], m["w3"]
+    wide_a, wide_b = 2 * wa, 2 * wb
+    for c in range(2):
+        half = slice(c * 128, c * 128 + 128)
+        flat[c, 96:128, :] = jnp.zeros((32, 128), F32)
+        flat[c, 0:wa, :] = rows_a[:, half].astype(F32)
+        flat[c, wa : wa + wb, :] = rows_b[:, half].astype(F32)
+        inT[c] = flat[c, 0:128, :].T.astype(BF).reshape(4, 32, 128)
+    w1[...] = f1[...].astype(BF)
+    place = lax.broadcasted_iota(jnp.int32, (256, LANE), 0)
+    lane = lax.broadcasted_iota(jnp.int32, (256, LANE), 1)
+    spread = jnp.zeros((8, 256), F32)
+    spread = spread + jnp.pad(marks_a[...].astype(F32), ((0, 0), (0, 256 - wide_a)))
+    spread = spread + jnp.concatenate(
+        [
+            jnp.zeros((8, wide_a), F32),
+            marks_b[...].astype(F32),
+            jnp.zeros((8, 256 - wide_a - wide_b), F32),
+        ],
+        axis=1,
+    )
+    for b in range(2):
+        pick = jnp.where(place == 2 * lane + b, 1.0, 0.0)
+        planes = dot_nn(spread.astype(BF), pick.astype(BF))
+        for a in range(2):
+            lab[2 * a + b : 2 * a + b + 1, :] = planes[a : a + 1, :]
+            lab[4 + 2 * a + b : 5 + 2 * a + b, :] = planes[2 + a : 3 + a, :]
+
     IN, LB = m["IN"], m["LB"]
     in_copies = []
     for dz in range(4):
-        for dx in range(2):
-            if dz == 0 and dx == 0:
+        zt = lax.rem(z + dz, 4)
+        for d in range(4):
+            if dz == 0 and d == 0:
                 continue
-            zt = lax.rem(z + dz, 4)
-            xt = lax.rem(x + dx, 2)
+            there = lax.rem(2 * x + y + d, 4)
             in_copies.append(
-                push(inT.at[span(xt, 128)], IN.at[2 * z + x, e], ha(zt, xt, e), y)
+                push(
+                    inT.at[:, there],
+                    IN.at[2 * z + x, e, pl.ds(2 * y, 2)],
+                    ha(zt, lax.div(there, 2), e),
+                    lax.rem(there, 2),
+                )
             )
-    IN[2 * z + x, e] = inT[span(x, 128), :]
+    IN[2 * z + x, e, pl.ds(2 * y, 2)] = inT[:, 2 * x + y]
 
     W1, W2, WU, W3 = m["W1"], m["W2"], m["WU"], m["W3"]
     b1 = reserve(4)
     for i in range(4):
         hand(
             w1.at[:, :, i * 128 : i * 128 + 128],
-            W1.at[:, span(2 * x + e, 32), :],
-            ha(2 * y + i // 2, lax.rem(z, 2), i % 2),
-            lax.div(z, 2),
+            W1.at[:, span(z, 32), :],
+            ha(2 * y + i // 2, x, i % 2),
+            e,
             b1 + i,
-            b1 + 2 * x + e,
+            b1 + z,
         )
     lab_copies = []
     LB[h] = lab[...]
@@ -527,6 +568,21 @@
         copy.wait_recv()
     twin_in = push(IN.at[:, e], IN.at[:, e], twin, y)
 
+    w2[...] = f2[...].astype(BF)
+    w3[...] = f3[...].astype(BF)
+    for k in range(4):
+        wu[k] = jnp.concatenate([fu[p, :, k * 64 : k * 64 + 64] for p in range(4)], axis=1).astype(BF)
+    for a in range(2):
+        for c in range(2):
+            half = slice(c * 128, c * 128 + 128)
+            buf = flat.at[2 * a + c]
+            buf[224:256, :] = jnp.zeros((32, 128), F32)
+            buf[0:wide_a, :] = skip_a[a, :, half].astype(F32)
+            buf[wide_a : wide_a + wide_b, :] = skip_b[a, :, half].astype(F32)
+            for b in range(2):
+                p = 2 * a + b
+                plane = buf[pl.ds(b, 128, stride=2), :]
+                skT[2 * c : 2 * c + 2, :, p * 128 : p * 128 + 128] = plane.T.astype(BF).reshape(2, 64, 128)
     b2 = reserve(2)
     for i in range(2):
         hand(
@@ -585,13 +641,20 @@
         landed(W1.at[:, 32 * j : 32 * j + 32, :], b1 + j)
     transposed(W1, m["W1T"], 128)
     twin_in.wait_recv()
-    X1, X2, X3 = m["X1"], m["X2"], m["X3"]
-    patches(lambda i: IN[lax.div(i, 2), lax.rem(i, 2)], X1)
+    X = m["X"]
+
+    def input_block(i):
+        return IN[lax.div(i, 2), lax.rem(i, 2)].reshape(128, 128)
+
+    def middle_block(i):
+        return A1[:, :, span(i, 128)].reshape(128, 128)
+
+    patches(input_block, X)
     P1, P1b, R1, A1 = m["P1"], m["P1b"], m["R1"], m["A1"]
 
     def conv_one(n, carry):
         cols = span(n, 512)
-        total = dot_nn(m["W1T"][...], X1[:, cols]).reshape(4, 32, 512)
+        total = dot_nn(m["W1T"][...], X[:, cols]).reshape(4, 32, 512)
         P1[:, :, cols] = total
         P1b[:, :, cols] = total.astype(BF)
         return carry
@@ -649,12 +712,12 @@
     transposed(W2, m["W2T"], 128)
     arrive(wait_one)
 
-    patches(lambda i: A1[:, :, span(i, 128)].reshape(128, 128), X2)
+    patches(middle_block, X)
     Z, P2b, T2, S2b, R2 = m["Z"], m["P2b"], m["T2"], m["S2b"], m["R2"]
 
     def conv_two(n, carry):
         cols = span(n, 512)
-        Z[0:256, cols] = dot_nn(m["W2T"][...], X2[:, cols])
+        Z[0:256, cols] = dot_nn(m["W2T"][...], X[:, cols])
         P2b[:, cols] = Z[span(1 - e, 128), cols].astype(BF)
         return carry
 
@@ -745,7 +808,7 @@
                 up, di = (a + da - 1) % 2, (a + da - 1) // 2
                 for db in range(3):
                     tap = da * 3 + db
-                    X3[tap * 128 : tap * 128 + 128, p * 512 : p * 512 + 512] = J[
+                    X[tap * 128 : tap * 128 + 128, p * 512 : p * 512 + 512] = J[
                         up, b + db, :, (1 + di) * 128 : (5 + di) * 128
                     ]
 
@@ -757,7 +820,7 @@
 
     def conv_three(n, carry):
         cols = span(n, 256)
-        Z[0:512, cols] = dot_nn(m["W3T"][...], X3[:, cols])
+        Z[0:512, cols] = dot_nn(m["W3T"][...], X[:, cols])
         for k in range(4):
             P3b[k, :, cols] = Z[span(2 * k + 1 - e, 64), cols].astype(BF)
         return carry
@@ -777,6 +840,7 @@
     arrive(scatter(S3b, R3))
     pre3, act3, LG = m["pre3"], m["act3"], m["LG"]
     wide = (64, LANE)
+    head = fh[span(slot, 64), :].astype(BF).astype(F32)
     h0 = jnp.broadcast_to(head[:, 0:1], wide)
     h1 = jnp.broadcast_to(head[:, 1:2], wide)
     for b in range(16):
@@ -913,7 +977,7 @@
     wait_seven = scatter(S7b, R7)
 
     def grad_three(t, carry):
-        GW3[t] = dot_nt(X3[span(t, 128), :], G3[...].reshape(512, 2048)).astype(BF)
+        GW3[t] = dot_nt(X[span(t, 128), :], G3[...].reshape(512, 2048)).astype(BF)
         return carry
 
     lax.fori_loop(0, 9, grad_three, 0)
@@ -955,6 +1019,7 @@
         ht = lax.rem(h + d, 16)
         gu_copies.append(push(GWU.at[ht], RGU.at[h], ht, y))
     RGU[h] = GWU[h]
+    patches(middle_block, X)
     arrive(g2_last)
 
     def back_two(n, carry):
@@ -987,7 +1052,7 @@
     wait_eight = scatter(P8b, R8)
 
     def grad_two(t, carry):
-        GW2[t] = dot_nt(X2[span(t, 128), :], G2[...].reshape(256, 2048)).astype(BF)
+        GW2[t] = dot_nt(X[span(t, 128), :], G2[...].reshape(256, 2048)).astype(BF)
         return carry
 
     lax.fori_loop(0, 9, grad_two, 0)
@@ -1012,10 +1077,11 @@
             bg2 + j,
             bg2 + x,
         )
+    patches(input_block, X)
     arrive(wait_g1)
 
     def grad_one(t, carry):
-        GW1[t] = dot_nt(X1[span(t, 128), :], G1[...].reshape(128, 2048)).astype(BF)
+        GW1[t] = dot_nt(X[span(t, 128), :], G1[...].reshape(128, 2048)).astype(BF)
         return carry
 
     lax.fori_loop(0, 9, grad_one, 0)
@@ -1025,7 +1091,7 @@
         hand(
             GW1.at[:, 32 * j : 32 * j + 32, :],
             RG1.at[:, :, span(r_low, 128)],
-            ha(q, j // 2, j % 2),
+            ha(j, x, y),
             lax.div(z, 2),
             bg1 + j,
             bg1 + r_low,
@@ -1044,10 +1110,14 @@
         )
     for copy in gu_copies:
         copy.wait_recv()
+    sums = []
     for k in range(4):
-        guo[k] = (RGU[k].astype(F32) + RGU[4 + k].astype(F32)) + (
-            RGU[8 + k].astype(F32) + RGU[12 + k].astype(F32)
+        sums.append(
+            (RGU[k].astype(F32) + RGU[4 + k].astype(F32))
+            + (RGU[8 + k].astype(F32) + RGU[12 + k].astype(F32))
         )
+    for p in range(4):
+        guo[p] = jnp.concatenate([part[:, p * 64 : p * 64 + 64] for part in sums], axis=1)
     for k in range(2):
         landed(RG2.at[:, :, 256 * k : 256 * k + 256], bg2 + k)
     g2o[...] = RG2[...]
@@ -1059,18 +1129,6 @@
             copy.wait_send()
         else:
             pl.when(when)(copy.wait_send)
-
-
-def parity_planes(rows):
-    _, two, across, chans = rows.shape
-    split = rows.reshape(two, across // 2, 2, chans)
-    return split.transpose(3, 0, 2, 1)
-
-
-def lane_blocks(first, second):
-    free = LANE - first.shape[-1] - second.shape[-1]
-    both = jnp.concatenate([first, second], axis=-1)
-    return jnp.pad(both, [(0, 0)] * (both.ndim - 1) + [(0, free)])
 
 
 def resident_body(
@@ -1098,18 +1156,10 @@
     moment_head,
     square_head,
 ):
-    slot = lax.rem(lax.axis_index("ha"), 4)
-    pixels = lane_blocks(input_a[0, 0].T, input_b[0, 0].T)
-    skips = lane_blocks(parity_planes(skip_a), parity_planes(skip_b)).reshape(4, 64, 512)
-    marks = jnp.concatenate(
-        [
-            lane_blocks(parity_planes(one[..., None]), parity_planes(two[..., None])).reshape(4, LANE)
-            for one, two in ((labels_a, labels_b), (valid_a, valid_b))
-        ]
-    ).astype(F32)
-    head_low = w_head.astype(BF).astype(F32)
-    head_own = jnp.pad(lax.dynamic_slice_in_dim(head_low, slot * 64, 64, 0), ((0, 0), (0, 126)))
-    upward = w_upward.astype(BF).reshape(4, 64, 4, 64).transpose(2, 1, 0, 3).reshape(4, 64, 256)
+    marks = [
+        jnp.pad(jnp.concatenate([label[0], usable[0]]), ((0, 4), (0, 0)))
+        for label, usable in ((labels_a, valid_a), (labels_b, valid_b))
+    ]
     vmem = pl.BlockSpec(memory_space=pltpu.VMEM)
     g1, g2, gu, g3, hd = pl.pallas_call(
         lambda *refs: fused((input_a.shape[2], input_b.shape[2]), *refs),
@@ -1120,26 +1170,28 @@
             jax.ShapeDtypeStruct((9, 64, 256), F32),
             jax.ShapeDtypeStruct((5, 8, 128), F32),
         ),
-        in_specs=[vmem] * 8,
+        in_specs=[vmem] * 11,
         out_specs=[vmem] * 5,
         scratch_shapes=[pltpu.VMEM(shape, kind) for _, shape, kind in SCRATCH]
         + [pltpu.SemaphoreType.DMA((COPIES,)), pltpu.SemaphoreType.DMA((COPIES,))],
         compiler_params=pltpu.CompilerParams(
-            has_side_effects=True, vmem_limit_bytes=60 * 1024 * 1024
+            has_side_effects=True, vmem_limit_bytes=56 * 1024 * 1024
         ),
     )(
-        pixels,
-        skips,
-        marks,
-        head_own,
-        w_enter.astype(BF).reshape(9, 32, 512),
-        w_middle.astype(BF).reshape(9, 64, 512),
-        upward,
-        w_merge.astype(BF).reshape(9, 64, 256),
+        input_a[0, 0],
+        input_b[0, 0],
+        skip_a[0],
+        skip_b[0],
+        *marks,
+        w_enter.reshape(9, 32, 512),
+        w_middle.reshape(9, 64, 512),
+        w_upward.reshape(4, 64, 256),
+        w_merge.reshape(9, 64, 256),
+        w_head,
     )
     grad_enter = g1.astype(F32).reshape(w_enter.shape)
     grad_middle = g2.astype(F32).reshape(w_middle.shape)
-    grad_upward = gu.reshape(4, 64, 4, 64).transpose(2, 1, 0, 3).reshape(w_upward.shape)
+    grad_upward = gu.reshape(w_upward.shape)
     grad_merge = g3.reshape(w_merge.shape)
     grad_head = hd[0:4, 0:2, 0:64].transpose(0, 2, 1).reshape(w_head.shape)
     return (

time: 276 us -> 242 us (0.88)
  the two profiles are of different devices: /device:TPU:3 before, /device:TPU:14 now
where the time goes in v2:
time: 242 us
  Pallas kernels  225 us (93%)
  other arithmetic  10.6 us (4%)
  local copies, waits for them, and re-layouts  5.36 us (2%)
    pallas_call x1, Pallas kernels, resident_body(): pl.pallas_call(lambda *refs: fused((input_a.shape[2], input_b.shape[2]),...  225 us
    convert_element_type x5, other arithmetic, adamw(): return (master_new, moment_new, square_new, master_new.astype(jnp.bfloat16))  9.14 us

profile of v2, /device:TPU:14, one launch (start us, length us, event | category | flops | bytes accessed | tf_op | source)
XLA Modules:
  0.0 241.6 jit_solution(5833024963300662137)
XLA Ops:
  0.7 1.5 copy.46.refs_10_
  2.1 0.7 pad_add_fusion
  2.8 0.6 pad.9.refs_5_
  3.4 0.7 pad_add_fusion.1
  4.1 0.6 pad.8.refs_4_
  4.7 0.0 copy-start.14
  4.8 0.0 copy-start.15
  4.8 0.0 copy-start.16
  4.8 0.0 copy-start
  4.8 0.0 copy-start.3
  4.8 224.9 %shard_map.390 = (bf16[9,32,512]{2,1,0:T(8,128)(2,1)}, bf16[9,64,512]{2,1,0:T(8,128)(2,1)}, f32[4,64,256]{2,1,0:T(8,128)}, f32[9,64,256]{2,1,0:T(8,128)}, f32[5,8,128]{2,1,0:T(8,128)}) custom-call(bf16[48,256]{1,0:T(8,128)(2,1)} %bitcast.35, bf16[72,256]{1,0:T(8,128)(2,1)} %bitcast.34, bf16[2,96,256]{2,1,0:T(8,128)(2,1)} %bitcast.33, ...), custom_call_target="tpu_custom_call" | custom-call | tf_op jit(solution)/shard_map/pallas_call | solution.py:1164
  229.7 0.7 slice_bitcast_fusion
  230.4 0.1 reshape.87
  230.5 0.0 copy-done.14
  230.5 0.0 copy-done.15
  230.5 0.0 copy-done.16
  230.5 0.6 fusion.7
  231.1 0.0 copy-done
  231.1 0.0 copy-done.3
  231.1 0.0 copy-start.1
  231.1 0.0 copy-start.5
  231.1 0.0 copy-start.6
  231.1 0.0 copy-start.7
  231.1 4.2 %fusion.13 = (bf16[3,3,64,512]{3,2,1,0:T(8,128)(2,1)}, f32[3,3,64,512]{3,2,1,0:T(8,128)}, f32[3,3,64,512]{3,2,1,0:T(8,128)}, f32[3,3,64,512]{3,2,1,0:T(8,128)}) fusion(f32[3,3,64,512]{3,2,1,0:T(8,128)S(1)} %copy-done, bf16[3,3,64,512]{3,2,1,0:T(8,128)(2,1)} %bitcast.29, f32[3,3,64,512]{3,2,1,0:T(8,128)S(1)} %copy-done.3, f32[3,3,64,512]{3,2,1,0:T(8,128)} %param.36), kind=kLoop, calls=%fused_computation.30 | loop fusion | flops 5013504 | bytes 8257536 | tf_op jit(solution)/shard_map/convert_element_type | solution.py:212
  235.4 0.0 copy-done.1
  235.4 0.0 copy-done.5
  235.4 0.0 copy-done.6
  235.4 0.0 copy-done.7
  235.4 0.0 copy-start.2
  235.4 0.0 copy-start.8
  235.4 0.0 copy-start.9
  235.5 0.0 copy-start.10
  235.5 1.6 fusion.9
  237.1 0.0 copy-done.2
  237.1 0.0 copy-done.8
  237.1 0.4 copy-done.9
  237.5 0.2 copy-done.10
  237.7 0.0 copy-start.4
  237.7 0.0 copy-start.11
  237.7 0.0 copy-start.12
  237.7 0.0 copy-start.13
  237.7 1.6 fusion.16
  239.3 0.0 copy-done.4
  239.3 0.0 copy-done.11
  239.3 0.0 copy-done.12
  239.3 0.0 copy-done.13
  239.3 1.0 fusion.11
  240.4 1.2 fusion.19
  (1 shorter events, 0.0 us)
Async XLA Ops:
  4.7 225.7 %copy-start.14 = (f32[256,2]{0,1:T(2,128)S(1)}, f32[256,2]{0,1:T(2,128)}, u32[]{:S(2)}) copy-start(f32[256,2]{0,1:T(2,128)} %param.43) | copy-start | bytes 6148
  4.8 225.7 %copy-start.15 = (f32[256,2]{0,1:T(2,128)S(1)}, f32[256,2]{0,1:T(2,128)}, u32[]{:S(2)}) copy-start(f32[256,2]{0,1:T(2,128)} %param.44) | copy-start | bytes 6148
  4.8 225.7 %copy-start.16 = (f32[256,2]{0,1:T(2,128)S(1)}, f32[256,2]{0,1:T(2,128)}, u32[]{:S(2)}) copy-start(f32[256,2]{0,1:T(2,128)} %param.45) | copy-start | bytes 6148
  4.8 226.3 %copy-start = (f32[3,3,64,512]{3,2,1,0:T(8,128)S(1)}, f32[3,3,64,512]{3,2,1,0:T(8,128)}, u32[]{:S(2)}) copy-start(f32[3,3,64,512]{3,2,1,0:T(8,128)} %param.34) | copy-start | bytes 3538948
  4.8 226.3 %copy-start.3 = (f32[3,3,64,512]{3,2,1,0:T(8,128)S(1)}, f32[3,3,64,512]{3,2,1,0:T(8,128)}, u32[]{:S(2)}) copy-start(f32[3,3,64,512]{3,2,1,0:T(8,128)} %param.35) | copy-start | bytes 3538948
  231.1 4.3 %copy-start.1 = (f32[3,3,64,256]{3,2,1,0:T(8,128)S(1)}, f32[3,3,64,256]{3,2,1,0:T(8,128)}, u32[]{:S(2)}) copy-start(f32[3,3,64,256]{3,2,1,0:T(8,128)} %param.40) | copy-start | bytes 1769476
  231.1 4.3 %copy-start.5 = (f32[3,3,64,256]{3,2,1,0:T(8,128)S(1)}, f32[3,3,64,256]{3,2,1,0:T(8,128)}, u32[]{:S(2)}) copy-start(f32[3,3,64,256]{3,2,1,0:T(8,128)} %param.41) | copy-start | bytes 1769476
  231.1 4.3 %copy-start.6 = (f32[3,3,64,256]{3,2,1,0:T(8,128)S(1)}, f32[3,3,64,256]{3,2,1,0:T(8,128)}, u32[]{:S(2)}) copy-start(f32[3,3,64,256]{3,2,1,0:T(8,128)} %param.42) | copy-start | bytes 1769476
  231.1 4.3 %copy-start.7 = (f32[9,64,256]{2,1,0:T(8,128)S(1)}, f32[9,64,256]{2,1,0:T(8,128)}, u32[]{:S(2)}) copy-start(f32[9,64,256]{2,1,0:T(8,128)} %get-tuple-element.30) | copy-start | bytes 1769476
  235.4 1.7 copy-start.2
  235.4 1.6 copy-start.8
  235.4 2.1 copy-start.9
  235.5 2.2 copy-start.10
  237.7 1.7 copy-start.4
  237.7 1.7 copy-start.11
  237.7 1.7 copy-start.12
  237.7 1.7 copy-start.13

commit v3 on v2

--- a/solution.py
+++ b/solution.py
@@ -372,28 +372,28 @@
     ("W2T", (256, 1152), BF),
     ("WUT", (256, 1024), BF),
     ("W3T", (512, 1152), BF),
-    ("X", (1152, 2048), BF),
+    ("X", (1152, 2304), BF),
     ("P1", (4, 32, 2048), F32),
     ("P1b", (4, 32, 2048), BF),
     ("R1", (3, 32, 2048), BF),
     ("A1", (4, 32, 2048), BF),
-    ("P2b", (128, 2048), BF),
-    ("T2", (128, 2048), BF),
-    ("S2b", (4, 128, 512), BF),
+    ("P2b", (4, 128, 512), BF),
+    ("T2", (4, 128, 512), BF),
+    ("S2b", (3, 128, 512), BF),
     ("R2", (3, 128, 512), BF),
     ("pre2", (128, 512), F32),
     ("A2", (8, 128, 512), BF),
     ("J", (2, 4, 128, 768), BF),
-    ("P3b", (4, 64, 2048), BF),
-    ("T3", (4, 64, 2048), BF),
-    ("S3b", (4, 64, 2048), BF),
-    ("R3", (3, 64, 2048), BF),
+    ("P3b", (4, 4, 64, 512), BF),
+    ("T3", (4, 4, 64, 512), BF),
+    ("S3b", (4, 4, 64, 512), BF),
+    ("R3", (4, 3, 64, 512), BF),
     ("pre3", (64, 2048), F32),
     ("act3", (64, 2048), BF),
     ("LG", (8, 32, 128), F32),
     ("LBL", (32, 128), F32),
     ("DL", (32, 128), F32),
-    ("G3", (8, 64, 2048), BF),
+    ("G3", (4, 8, 64, 512), BF),
     ("Z", (1152, 2048), F32),
     ("HS", (2, 2, 64, 128), F32),
     ("HR", (2, 2, 64, 128), F32),
@@ -413,19 +413,20 @@
     ("GW2", (9, 128, 256), BF),
     ("GW1", (9, 128, 128), BF),
     ("RG3", (4, 9, 64, 256), BF),
+    ("Y3", (2, 9, 64, 256), BF),
     ("RGU", (16, 64, 256), BF),
     ("RG2", (9, 64, 512), BF),
     ("RG1", (9, 32, 512), BF),
     ("HD", (16, 8, 128), F32),
 )
-COPIES = 176
+COPIES = 216
 
 
 def fused(widths, *refs):
     wa, wb = widths
-    rows_a, rows_b, skip_a, skip_b, marks_a, marks_b, f1, f2, fu, f3, fh = refs[:11]
-    g1o, g2o, guo, g3o, hdo = refs[11:16]
-    m = {name: ref for (name, _, _), ref in zip(SCRATCH, refs[16:-2])}
+    rows_a, rows_b, skip_a, skip_b, la, lb, va, vb, f1, f2, fu, f3, fh = refs[:13]
+    g1o, g2o, guo, g3o, hdo = refs[13:18]
+    m = {name: ref for (name, _, _), ref in zip(SCRATCH, refs[18:-2])}
     send_sem, recv_sem = refs[-2:]
     h, y = lax.axis_index("ha"), lax.axis_index("col")
     z, x, e = lax.div(h, 4), lax.rem(lax.div(h, 2), 2), lax.rem(h, 2)
@@ -513,16 +514,14 @@
     w1[...] = f1[...].astype(BF)
     place = lax.broadcasted_iota(jnp.int32, (256, LANE), 0)
     lane = lax.broadcasted_iota(jnp.int32, (256, LANE), 1)
-    spread = jnp.zeros((8, 256), F32)
-    spread = spread + jnp.pad(marks_a[...].astype(F32), ((0, 0), (0, 256 - wide_a)))
-    spread = spread + jnp.concatenate(
+    spread = jnp.concatenate(
         [
-            jnp.zeros((8, wide_a), F32),
-            marks_b[...].astype(F32),
-            jnp.zeros((8, 256 - wide_a - wide_b), F32),
+            jnp.concatenate([first[...], second[...]], axis=1).astype(F32)
+            for first, second in ((la, lb), (va, vb))
         ],
-        axis=1,
-    )
+        axis=0,
+    )
+    spread = jnp.pad(spread, ((0, 4), (0, 256 - wide_a - wide_b)))
     for b in range(2):
         pick = jnp.where(place == 2 * lane + b, 1.0, 0.0)
         planes = dot_nn(spread.astype(BF), pick.astype(BF))
@@ -616,22 +615,28 @@
             b3 + 2 * lax.div(z, 2) + y,
         )
 
-    def patches(block, out):
+    X = m["X"]
+
+    def patch_edges():
+        zero = jnp.zeros((384, 128), BF)
+        X[0:384, 128:256] = zero
+        X[768:1152, 2048:2176] = zero
+
+    def patches(block, first, last):
         def one(i, carry):
             low = block(i)
             v = low.astype(F32)
             kinds = (from_left(v).astype(BF), low, from_right(v).astype(BF))
             for di in (-1, 0, 1):
-                row = lax.rem(i - di + 16, 16)
                 for dj in range(3):
                     tap = (di + 1) * 3 + dj
-                    out[tap * 128 : tap * 128 + 128, span(row, 128)] = kinds[dj]
+                    X[tap * 128 : tap * 128 + 128, span(i - di + 1, 128)] = kinds[dj]
             return carry
 
-        lax.fori_loop(0, 16, one, 0)
-        zero = jnp.zeros((384, 128), BF)
-        out[0:384, 0:128] = zero
-        out[768:1152, 1920:2048] = zero
+        lax.fori_loop(first, last, one, 0)
+
+    def patch_cols(at, size):
+        return pl.ds(pl.multiple_of(at * size + 128, 128), size)
 
     def transposed(weight, out, rows):
         for t in range(weight.shape[0]):
@@ -641,7 +646,6 @@
         landed(W1.at[:, 32 * j : 32 * j + 32, :], b1 + j)
     transposed(W1, m["W1T"], 128)
     twin_in.wait_recv()
-    X = m["X"]
 
     def input_block(i):
         return IN[lax.div(i, 2), lax.rem(i, 2)].reshape(128, 128)
@@ -649,53 +653,64 @@
     def middle_block(i):
         return A1[:, :, span(i, 128)].reshape(128, 128)
 
-    patches(input_block, X)
+    patches(input_block, 0, 16)
+    patch_edges()
     P1, P1b, R1, A1 = m["P1"], m["P1b"], m["R1"], m["A1"]
 
     def conv_one(n, carry):
         cols = span(n, 512)
-        total = dot_nn(m["W1T"][...], X[:, cols]).reshape(4, 32, 512)
+        total = dot_nn(m["W1T"][...], X[:, patch_cols(n, 512)]).reshape(4, 32, 512)
         P1[:, :, cols] = total
         P1b[:, :, cols] = total.astype(BF)
         return carry
 
-    lax.fori_loop(0, 4, conv_one, 0)
-
     def to_plane(d):
         there = lax.rem(q + d, 4)
         return there, ha(z, lax.rem(there, 2), e), lax.div(there, 2)
 
-    def scatter(source, slots):
+    def scatter(source, slots, cols=slice(None)):
         copies = []
         for d in range(1, 4):
             there, h2, y2 = to_plane(d)
-            copies.append(push(source.at[there], slots.at[d - 1], h2, y2))
+            copies.append(push(source.at[there, :, cols], slots.at[d - 1, :, cols], h2, y2))
         return copies
 
-    def gather_four(buf):
+    def gather_four(buf, cols):
         copies = []
         for d in range(1, 4):
             _, h2, y2 = to_plane(d)
-            copies.append(push(buf.at[q], buf.at[q], h2, y2))
+            copies.append(push(buf.at[q, :, cols], buf.at[q, :, cols], h2, y2))
         return copies
 
-    def gather_plane(buf):
+    halves = (slice(0, 1024), slice(1024, 2048))
+
+    def plane_sends(buf):
         copies = []
         for d in range(1, 4):
             _, h2, y2 = to_plane(d)
             copies.append(push(buf.at[s], buf.at[s], h2, y2))
-        last = [push(buf.at[s], buf.at[s], twin, y)]
+        return copies, push(buf.at[s], buf.at[s], twin, y)
+
+    def plane_passes(buf, sends):
+        copies, own = sends
+        last = [own]
         for d in range(1, 4):
             copies[d - 1].wait_recv()
             came = 2 * lax.rem(q + 4 - d, 4) + e
             last.append(push(buf.at[came], buf.at[came], twin, y))
         return last
 
+    def gather_plane(buf):
+        return plane_passes(buf, plane_sends(buf))
+
     def arrive(copies):
         for copy in copies:
             copy.wait_recv()
 
-    arrive(scatter(P1b, R1))
+    one_out = []
+    for c in range(2):
+        lax.fori_loop(2 * c, 2 * c + 2, conv_one, 0)
+        one_out.append(scatter(P1b, R1, halves[c]))
 
     def act_one(n, carry):
         cols = span(n, 512)
@@ -705,44 +720,46 @@
         A1[q, :, cols] = gelu_value(total).astype(BF)
         return carry
 
-    lax.fori_loop(0, 4, act_one, 0)
-    wait_one = gather_four(A1)
+    wait_one = []
+    for c in range(2):
+        arrive(one_out[c])
+        lax.fori_loop(2 * c, 2 * c + 2, act_one, 0)
+        wait_one.append(gather_four(A1, halves[c]))
     for j in range(2):
         landed(W2.at[:, 64 * j : 64 * j + 64, :], b2 + j)
     transposed(W2, m["W2T"], 128)
-    arrive(wait_one)
-
-    patches(middle_block, X)
+
+    for c in range(2):
+        arrive(wait_one[c])
+        patches(middle_block, 8 * c, 8 * c + 8)
+    patch_edges()
     Z, P2b, T2, S2b, R2 = m["Z"], m["P2b"], m["T2"], m["S2b"], m["R2"]
 
-    def conv_two(n, carry):
-        cols = span(n, 512)
-        Z[0:256, cols] = dot_nn(m["W2T"][...], X[:, cols])
-        P2b[:, cols] = Z[span(1 - e, 128), cols].astype(BF)
-        return carry
-
-    lax.fori_loop(0, 4, conv_two, 0)
-    arrive([push(P2b, T2, twin, y)])
-
-    def pair_two(n, carry):
-        cols = span(n, 512)
-        total = Z[span(e, 128), cols] + T2[:, cols].astype(F32)
-        Z[span(e, 128), cols] = total
-        S2b[n] = total.astype(BF)
-        return carry
-
-    lax.fori_loop(0, 4, pair_two, 0)
-    two = []
-    for d in range(1, 4):
-        zt = lax.rem(z + d, 4)
-        two.append(push(S2b.at[zt], R2.at[d - 1], ha(zt, x, e), y))
+    def band_two(k):
+        zt = lax.rem(z + 1 + k, 4)
+        Z[0:256, span(zt, 512)] = dot_nn(m["W2T"][...], X[:, patch_cols(zt, 512)])
+        P2b[k] = Z[span(1 - e, 128), span(zt, 512)].astype(BF)
+        return push(P2b.at[k], T2.at[k], twin, y)
+
+    def pair_two(k):
+        zt = lax.rem(z + 1 + k, 4)
+        pairs[k].wait_recv()
+        S2b[k] = (Z[span(e, 128), span(zt, 512)] + T2[k].astype(F32)).astype(BF)
+        two.append(push(S2b.at[k], R2.at[k], ha(zt, x, e), y))
+
+    pairs, two = [], []
+    for k in range(4):
+        pairs.append(band_two(k))
+        if k >= 1:
+            pair_two(k - 1)
     for d in range(1, 16):
         bu_copies[d - 1].wait_recv()
     for t in range(8):
         m["WUT"][:, t * 128 : t * 128 + 128] = WU[2 * t : 2 * t + 2].reshape(128, 256).T
     arrive(two)
     pre2, A2 = m["pre2"], m["A2"]
-    total = Z[span(e, 128), span(z, 512)] + R2[0].astype(F32)
+    pairs[3].wait_recv()
+    total = Z[span(e, 128), span(z, 512)] + T2[3].astype(F32) + R2[0].astype(F32)
     total = total + R2[1].astype(F32) + R2[2].astype(F32)
     pre2[...] = total
     A2[s] = gelu_value(total).astype(BF)
@@ -760,7 +777,7 @@
         plane = dot_nn(m["WUT"][p * 64 : p * 64 + 64, :], A2[...].reshape(1024, 512))
         J[p // 2, 1 + p % 2, 0:64, 128:640] = plane.astype(BF)
 
-    def fringe(part, up, down, send_down, keep_down, send_up, keep_up):
+    def fringe(up, down, send_down, keep_down, send_up, keep_up):
         below = remote(send_down, keep_down, lax.rem(h + 4, 16), y, down, down)
         above = remote(send_up, keep_up, lax.rem(h + 12, 16), y, up, up)
 
@@ -787,30 +804,46 @@
         return wait
 
     bj = reserve(2)
-    fringe(
-        None,
+    wait_rows = fringe(
         bj,
         bj + 1,
         J.at[1, 1:3, :, 512:640],
         J.at[1, 1:3, :, 0:128],
         J.at[0, 1:3, :, 128:256],
         J.at[0, 1:3, :, 640:768],
-    )()
-    for a in range(2):
-        for i in range(1 - a, 6 - a):
-            at = slice(i * 128, i * 128 + 128)
-            J[a, 0, :, at] = from_left(J[a, 2, :, at].astype(F32)).astype(BF)
-            J[a, 3, :, at] = from_right(J[a, 1, :, at].astype(F32)).astype(BF)
-    for a in range(2):
-        for b in range(2):
-            p = 2 * a + b
+    )
+
+    def beside(a, i):
+        at = slice(i * 128, i * 128 + 128)
+        J[a, 0, :, at] = from_left(J[a, 2, :, at].astype(F32)).astype(BF)
+        J[a, 3, :, at] = from_right(J[a, 1, :, at].astype(F32)).astype(BF)
+
+    def joined_patches(outer):
+        for a in range(2):
             for da in range(3):
                 up, di = (a + da - 1) % 2, (a + da - 1) // 2
-                for db in range(3):
-                    tap = da * 3 + db
-                    X[tap * 128 : tap * 128 + 128, p * 512 : p * 512 + 512] = J[
-                        up, b + db, :, (1 + di) * 128 : (5 + di) * 128
-                    ]
+                first, last = 0, 4
+                if di != 0:
+                    edge = 0 if di < 0 else 3
+                    first, last = (edge, edge + 1) if outer else (1, 4) if di < 0 else (0, 3)
+                elif outer:
+                    continue
+                for b in range(2):
+                    for db in range(3):
+                        tap = da * 3 + db
+                        at = 128 + (2 * a + b) * 512
+                        X[tap * 128 : tap * 128 + 128, at + first * 128 : at + last * 128] = J[
+                            up, b + db, :, (1 + di + first) * 128 : (1 + di + last) * 128
+                        ]
+
+    for a in range(2):
+        for i in range(1, 5):
+            beside(a, i)
+    joined_patches(False)
+    wait_rows()
+    beside(1, 0)
+    beside(0, 5)
+    joined_patches(True)
 
     for j in range(4):
         t, half = j // 2, j % 2
@@ -818,42 +851,55 @@
     transposed(W3, m["W3T"], 128)
     P3b, T3, S3b, R3 = m["P3b"], m["T3"], m["S3b"], m["R3"]
 
-    def conv_three(n, carry):
-        cols = span(n, 256)
-        Z[0:512, cols] = dot_nn(m["W3T"][...], X[:, cols])
+    def plane_three(p):
+        def step(n, carry):
+            Z[0:512, span(n, 256)] = dot_nn(m["W3T"][...], X[:, patch_cols(n, 256)])
+            return carry
+
+        lax.fori_loop(2 * p, 2 * p + 2, step, 0)
+        cols = slice(p * 512, p * 512 + 512)
         for k in range(4):
-            P3b[k, :, cols] = Z[span(2 * k + 1 - e, 64), cols].astype(BF)
-        return carry
-
-    lax.fori_loop(0, 8, conv_three, 0)
-    arrive([push(P3b, T3, twin, y)])
-
-    def pair_three(n, carry):
-        cols = span(n, 512)
+            P3b[p, k] = Z[span(2 * k + 1 - e, 64), cols].astype(BF)
+        return push(P3b.at[p], T3.at[p], twin, y)
+
+    def pair_three(p):
+        pairs[p].wait_recv()
+        cols = slice(p * 512, p * 512 + 512)
         for k in range(4):
-            total = Z[span(2 * k + e, 64), cols] + T3[k, :, cols].astype(F32)
+            total = Z[span(2 * k + e, 64), cols] + T3[p, k].astype(F32)
             Z[span(2 * k + e, 64), cols] = total
-            S3b[k, :, cols] = total.astype(BF)
-        return carry
-
-    lax.fori_loop(0, 4, pair_three, 0)
-    arrive(scatter(S3b, R3))
+            S3b[p, k] = total.astype(BF)
+        three.append(scatter(S3b.at[p], R3.at[p]))
+
+    pairs, three = [], []
+    for p in range(4):
+        pairs.append(plane_three(p))
+        if p >= 1:
+            pair_three(p - 1)
+    pair_three(3)
     pre3, act3, LG = m["pre3"], m["act3"], m["LG"]
     wide = (64, LANE)
     head = fh[span(slot, 64), :].astype(BF).astype(F32)
     h0 = jnp.broadcast_to(head[:, 0:1], wide)
     h1 = jnp.broadcast_to(head[:, 1:2], wide)
     for b in range(16):
+        if b % 4 == 0:
+            arrive(three[b // 4])
         cols = slice(b * 128, b * 128 + 128)
-        total = Z[span(s, 64), cols] + R3[0, :, cols].astype(F32)
-        total = total + R3[1, :, cols].astype(F32) + R3[2, :, cols].astype(F32)
+        part = slice(b % 4 * 128, b % 4 * 128 + 128)
+        total = Z[span(s, 64), cols] + R3[b // 4, 0, :, part].astype(F32)
+        total = total + R3[b // 4, 1, :, part].astype(F32) + R3[b // 4, 2, :, part].astype(F32)
         pre3[:, cols] = total
         act = gelu_value(total).astype(BF)
         act3[:, cols] = act
         act = act.astype(F32)
         LG[s, b : b + 1, :] = jnp.sum(act * h0, axis=0, keepdims=True)
         LG[s, 16 + b : 17 + b, :] = jnp.sum(act * h1, axis=0, keepdims=True)
-    wait_logits = gather_plane(LG)
+    wait_logits = []
+    for d in range(1, 8):
+        there = lax.rem(s + d, 8)
+        half = lax.div(there, 4)
+        wait_logits.append(push(LG.at[s], LG.at[s], 4 * z + there - 4 * half, half))
     for copy in lab_copies:
         copy.wait_recv()
     LBL = m["LBL"]
@@ -884,17 +930,20 @@
     DL[16:32, :] = jnp.where(picks, own, other).astype(BF).astype(F32)
     loss = jnp.sum(jnp.sum(terms, axis=0, keepdims=True), axis=1, keepdims=True)
     G3, HD = m["G3"], m["HD"]
+    planes = []
     sum0 = jnp.zeros(wide, F32)
     sum1 = jnp.zeros(wide, F32)
     for b in range(16):
         cols = slice(b * 128, b * 128 + 128)
         d0 = jnp.broadcast_to(DL[b : b + 1, :], wide)
         d1 = jnp.broadcast_to(DL[16 + b : 17 + b, :], wide)
-        G3[s, :, cols] = ((h0 * d0 + h1 * d1) * gelu_slope(pre3[:, cols])).astype(BF)
+        part = slice(b % 4 * 128, b % 4 * 128 + 128)
+        G3[b // 4, s, :, part] = ((h0 * d0 + h1 * d1) * gelu_slope(pre3[:, cols])).astype(BF)
         act = act3[:, cols].astype(F32)
         sum0 = sum0 + act * d0
         sum1 = sum1 + act * d1
-    wait_g3 = gather_plane(G3)
+        if b % 4 == 3:
+            planes.append(plane_sends(G3.at[b // 4]))
     side = lax.broadcasted_iota(jnp.int32, wide, 1)
     sum0 = jnp.sum(sum0, axis=1, keepdims=True)
     sum1 = jnp.sum(sum1, axis=1, keepdims=True)
@@ -904,18 +953,19 @@
     hd_copies = []
     for d in range(1, 16):
         hd_copies.append(push(HD.at[h], HD.at[h], lax.rem(h + d, 16), y))
-    arrive(wait_g3)
 
     HS, DB, DR = m["HS"], m["DB"], m["DR"]
 
-    def back_three(n, carry):
-        cols = span(n, 256)
-        Z[0:576, cols] = dot_nn(
-            W3[:, 0:64, :].reshape(576, 512), G3[:, :, cols].reshape(512, 256)
-        )
-        return carry
-
-    lax.fori_loop(0, 8, back_three, 0)
+    def back_three(p):
+        grads = G3[p].reshape(512, 512)
+        Z[0:576, p * 512 : p * 512 + 512] = dot_nn(W3[:, 0:64, :].reshape(576, 512), grads)
+
+    passes = [plane_passes(G3.at[0], planes[0])]
+    for p in range(4):
+        if p < 3:
+            passes.append(plane_passes(G3.at[p + 1], planes[p + 1]))
+        arrive(passes[p])
+        back_three(p)
     ways = (((0, 0, 0), (1, -1, 0), (1, 1, 1)), ((0, -1, -1), (0, 1, 0), (1, 0, 0)))
 
     def raised_block(a, b, i):
@@ -936,7 +986,7 @@
         HS[0, b] = raised_block(0, b, 4)
         HS[1, b] = raised_block(1, b, -1)
     bh = reserve(2)
-    wait_fringe = fringe(None, bh, bh + 1, HS.at[0], HR.at[0], HS.at[1], HR.at[1])
+    wait_fringe = fringe(bh, bh + 1, HS.at[0], HR.at[0], HS.at[1], HR.at[1])
     for a in range(2):
         for b in range(2):
             p = 2 * a + b
@@ -946,6 +996,18 @@
                     DB[p] = block
                 else:
                     DR[p * 64 : p * 64 + 64, i * 128 : i * 128 + 128] = block.astype(BF)
+    GW3, GWU, GW2, GW1 = m["GW3"], m["GWU"], m["GW2"], m["GW1"]
+    RG3, RGU, RG2, RG1 = m["RG3"], m["RGU"], m["RG2"], m["RG1"]
+
+    def grad_three(t, carry):
+        total = None
+        for p in range(4):
+            part = dot_nt(X[span(t, 128), 128 + p * 512 : 640 + p * 512], G3[p].reshape(512, 512))
+            total = part if total is None else total + part
+        GW3[t] = total.astype(BF)
+        return carry
+
+    lax.fori_loop(0, 3, grad_three, 0)
     wait_fringe()
     for a in range(2):
         for b in range(2):
@@ -963,24 +1025,17 @@
         P7b[k] = Z[span(2 * k + 1 - e, 128), 0:512].astype(BF)
     wait_pair = push(P7b, T7, twin, y)
 
-    GW3, GWU, GW2, GW1 = m["GW3"], m["GWU"], m["GW2"], m["GW1"]
-    RG3, RGU, RG2, RG1 = m["RG3"], m["RGU"], m["RG2"], m["RG1"]
-
     def pair_seven():
         for k in range(4):
             total = Z[span(2 * k + e, 128), 0:512] + T7[k].astype(F32)
             Z[span(2 * k + e, 128), 0:512] = total
             S7b[k] = total.astype(BF)
 
+    lax.fori_loop(3, 5, grad_three, 0)
     wait_pair.wait_recv()
     pair_seven()
     wait_seven = scatter(S7b, R7)
-
-    def grad_three(t, carry):
-        GW3[t] = dot_nt(X[span(t, 128), :], G3[...].reshape(512, 2048)).astype(BF)
-        return carry
-
-    lax.fori_loop(0, 9, grad_three, 0)
+    lax.fori_loop(5, 9, grad_three, 0)
 
     def grad_up(k, carry):
         GWU[pl.ds(2 * k, 2)] = dot_nt(A2[k], DR[...]).astype(BF).reshape(2, 64, 256)
@@ -997,21 +1052,49 @@
     for d in range(1, 4):
         zt = lax.rem(z + d, 4)
         g2_copies.append(push(mine, mine, ha(zt, x, e), y))
-    g2_last = [push(mine, mine, twin, y)]
-    for d in range(1, 4):
+    own_pair = push(mine, mine, twin, y)
+    Y3 = m["Y3"]
+    other = 1 - y
+    across = []
+    for t in range(2):
+        across.append(
+            push(
+                GW3.at[:, 64 * t : 64 * t + 64, span(other, 256)],
+                Y3.at[t],
+                h,
+                other,
+            )
+        )
+    patches(middle_block, 0, 16)
+    patch_edges()
+
+    def back_two(zs):
+        for k in range(2):
+            cols = pl.ds(pl.multiple_of(zs * 512 + k * 256, 256), 256)
+            Z[:, cols] = dot_nn(W2[...].reshape(1152, 256), G2[:, :, cols].reshape(256, 256))
+
+    def relay(d):
         g2_copies[d - 1].wait_recv()
-        came = G2.at[e, :, span(lax.rem(z + 4 - d, 4), 512)]
-        g2_last.append(push(came, came, twin, y))
-
+        zs = lax.rem(z + 4 - d, 4)
+        came = G2.at[e, :, span(zs, 512)]
+        return zs, push(came, came, twin, y)
+
+    zs, copy = relay(1)
+    own_pair.wait_recv()
+    back_two(z)
+    for d in range(2, 4):
+        after = relay(d)
+        copy.wait_recv()
+        back_two(zs)
+        zs, copy = after
     bg3 = reserve(4)
-    for j in range(4):
-        t, half = j // 2, j % 2
+    for t in range(2):
         hand(
-            GW3.at[:, 64 * t : 64 * t + 64, 256 * half : 256 * half + 256],
+            GW3.at[:, 64 * t : 64 * t + 64, span(y, 256)],
             RG3.at[z],
             ha(2 * t + y, x, e),
-            half,
-            bg3 + j,
+            y,
+            bg3 + t,
             bg3 + z,
         )
     gu_copies = []
@@ -1019,15 +1102,8 @@
         ht = lax.rem(h + d, 16)
         gu_copies.append(push(GWU.at[ht], RGU.at[h], ht, y))
     RGU[h] = GWU[h]
-    patches(middle_block, X)
-    arrive(g2_last)
-
-    def back_two(n, carry):
-        cols = span(n, 256)
-        Z[:, cols] = dot_nn(W2[...].reshape(1152, 256), G2[:, :, cols].reshape(256, 256))
-        return carry
-
-    lax.fori_loop(0, 8, back_two, 0)
+    copy.wait_recv()
+    back_two(zs)
     P8b, R8, G1 = m["P8b"], m["R8"], m["G1"]
     P8 = m["P8"]
 
@@ -1048,15 +1124,26 @@
         P8b[:, :, span(i, 128)] = total.reshape(4, 32, 128).astype(BF)
         return carry
 
-    lax.fori_loop(0, 16, fold, 0)
-    wait_eight = scatter(P8b, R8)
+    wait_eight = []
+    for c in range(2):
+        lax.fori_loop(8 * c, 8 * c + 8, fold, 0)
+        wait_eight.append(scatter(P8b, R8, halves[c]))
+    arrive(across)
+    for t in range(2):
+        hand(
+            Y3.at[t],
+            RG3.at[z],
+            ha(2 * t + other, x, e),
+            y,
+            bg3 + 2 + t,
+            bg3 + z,
+        )
 
     def grad_two(t, carry):
-        GW2[t] = dot_nt(X[span(t, 128), :], G2[...].reshape(256, 2048)).astype(BF)
+        GW2[t] = dot_nt(X[span(t, 128), 128:2176], G2[...].reshape(256, 2048)).astype(BF)
         return carry
 
     lax.fori_loop(0, 9, grad_two, 0)
-    arrive(wait_eight)
 
     def act_back(n, carry):
         cols = span(n, 512)
@@ -1065,8 +1152,11 @@
         G1[q, :, cols] = (total * gelu_slope(P1[q, :, cols])).astype(BF)
         return carry
 
-    lax.fori_loop(0, 4, act_back, 0)
-    wait_g1 = gather_four(G1)
+    wait_g1 = []
+    for c in range(2):
+        arrive(wait_eight[c])
+        lax.fori_loop(2 * c, 2 * c + 2, act_back, 0)
+        wait_g1 += gather_four(G1, halves[c])
     bg2 = reserve(2)
     for j in range(2):
         hand(
@@ -1077,11 +1167,12 @@
             bg2 + j,
             bg2 + x,
         )
-    patches(input_block, X)
+    patches(input_block, 0, 16)
+    patch_edges()
     arrive(wait_g1)
 
     def grad_one(t, carry):
-        GW1[t] = dot_nt(X[span(t, 128), :], G1[...].reshape(128, 2048)).astype(BF)
+        GW1[t] = dot_nt(X[span(t, 128), 128:2176], G1[...].reshape(128, 2048)).astype(BF)
         return carry
 
     lax.fori_loop(0, 9, grad_one, 0)
@@ -1156,10 +1247,6 @@
     moment_head,
     square_head,
 ):
-    marks = [
-        jnp.pad(jnp.concatenate([label[0], usable[0]]), ((0, 4), (0, 0)))
-        for label, usable in ((labels_a, valid_a), (labels_b, valid_b))
-    ]
     vmem = pl.BlockSpec(memory_space=pltpu.VMEM)
     g1, g2, gu, g3, hd = pl.pallas_call(
         lambda *refs: fused((input_a.shape[2], input_b.shape[2]), *refs),
@@ -1170,7 +1257,7 @@
             jax.ShapeDtypeStruct((9, 64, 256), F32),
             jax.ShapeDtypeStruct((5, 8, 128), F32),
         ),
-        in_specs=[vmem] * 11,
+        in_specs=[vmem] * 13,
         out_specs=[vmem] * 5,
         scratch_shapes=[pltpu.VMEM(shape, kind) for _, shape, kind in SCRATCH]
         + [pltpu.SemaphoreType.DMA((COPIES,)), pltpu.SemaphoreType.DMA((COPIES,))],
@@ -1182,7 +1269,10 @@
         input_b[0, 0],
         skip_a[0],
         skip_b[0],
-        *marks,
+        labels_a[0],
+        labels_b[0],
+        valid_a[0],
+        valid_b[0],
         w_enter.reshape(9, 32, 512),
         w_middle.reshape(9, 64, 512),
         w_upward.reshape(4, 64, 256),

time: 242 us -> 220 us (0.909)
  Pallas kernels: 225 us -> 205 us
    pallas_call x1, Pallas kernels: 225 us -> 205 us  [resident_body(): pl.pallas_call(lambda *refs: fused((input_a.shape[2], input_b.shape[2]),...]
where the time goes in v3:
time: 220 us; the launch traced here: 219 us
  Pallas kernels  205 us (93%)
  other arithmetic  9.14 us (4%)
  local copies, waits for them, and re-layouts  4.16 us (2%)
    pallas_call x1, Pallas kernels, resident_body(): pl.pallas_call(lambda *refs: fused((input_a.shape[2], input_b.shape[2]),...  205 us
    convert_element_type x5, other arithmetic, adamw(): return (master_new, moment_new, square_new, master_new.astype(jnp.bfloat16))  9.14 us

profile of v3, /device:TPU:14, one launch (start us, length us, event | category | flops | bytes accessed | tf_op | source)
XLA Modules:
  0.0 219.2 jit_solution(11426063403721717886)
XLA Ops:
  0.7 1.5 copy.46.refs_12_
  2.1 0.0 copy-start.14
  2.1 0.0 copy-start.15
  2.1 0.0 copy-start.16
  2.1 0.0 copy-start
  2.1 0.0 copy-start.3
  2.2 205.2 %shard_map.390 = (bf16[9,32,512]{2,1,0:T(8,128)(2,1)}, bf16[9,64,512]{2,1,0:T(8,128)(2,1)}, f32[4,64,256]{2,1,0:T(8,128)}, f32[9,64,256]{2,1,0:T(8,128)}, f32[5,8,128]{2,1,0:T(8,128)}) custom-call(bf16[48,256]{1,0:T(8,128)(2,1)} %bitcast.35, bf16[72,256]{1,0:T(8,128)(2,1)} %bitcast.34, bf16[2,96,256]{2,1,0:T(8,128)(2,1)} %bitcast.33, ...), custom_call_target="tpu_custom_call" | custom-call | tf_op jit(solution)/shard_map/pallas_call | solution.py:1251
  207.3 0.7 slice_bitcast_fusion
  208.0 0.1 reshape.87
  208.1 0.0 copy-done.14
  208.1 0.0 copy-done.15
  208.1 0.0 copy-done.16
  208.1 0.6 fusion.7
  208.7 0.0 copy-done
  208.7 0.0 copy-done.3
  208.8 0.0 copy-start.1
  208.8 0.0 copy-start.5
  208.8 0.0 copy-start.6
  208.8 0.0 copy-start.7
  208.8 4.2 %fusion.13 = (bf16[3,3,64,512]{3,2,1,0:T(8,128)(2,1)}, f32[3,3,64,512]{3,2,1,0:T(8,128)}, f32[3,3,64,512]{3,2,1,0:T(8,128)}, f32[3,3,64,512]{3,2,1,0:T(8,128)}) fusion(f32[3,3,64,512]{3,2,1,0:T(8,128)S(1)} %copy-done, bf16[3,3,64,512]{3,2,1,0:T(8,128)(2,1)} %bitcast.29, f32[3,3,64,512]{3,2,1,0:T(8,128)S(1)} %copy-done.3, f32[3,3,64,512]{3,2,1,0:T(8,128)} %param.36), kind=kLoop, calls=%fused_computation.28 | loop fusion | flops 5013504 | bytes 8257536 | tf_op jit(solution)/shard_map/convert_element_type | solution.py:212
  213.0 0.0 copy-done.1
  213.0 0.0 copy-done.5
  213.0 0.0 copy-done.6
  213.1 0.0 copy-done.7
  213.1 0.0 copy-start.2
  213.1 0.0 copy-start.8
  213.1 0.0 copy-start.9
  213.1 0.0 copy-start.10
  213.1 1.6 fusion.9
  214.7 0.0 copy-done.2
  214.7 0.0 copy-done.8
  214.7 0.4 copy-done.9
  215.2 0.2 copy-done.10
  215.3 0.0 copy-start.4
  215.3 0.0 copy-start.11
  215.3 0.0 copy-start.12
  215.3 0.0 copy-start.13
  215.3 1.6 fusion.16
  217.0 0.0 copy-done.4
  217.0 0.0 copy-done.11
  217.0 0.0 copy-done.12
  217.0 0.0 copy-done.13
  217.0 1.0 fusion.11
  218.0 1.2 fusion.19
  (1 shorter events, 0.0 us)
Async XLA Ops:
  2.1 206.0 %copy-start.14 = (f32[256,2]{0,1:T(2,128)S(1)}, f32[256,2]{0,1:T(2,128)}, u32[]{:S(2)}) copy-start(f32[256,2]{0,1:T(2,128)} %param.43) | copy-start | bytes 6148
  2.1 206.0 %copy-start.15 = (f32[256,2]{0,1:T(2,128)S(1)}, f32[256,2]{0,1:T(2,128)}, u32[]{:S(2)}) copy-start(f32[256,2]{0,1:T(2,128)} %param.44) | copy-start | bytes 6148
  2.1 206.0 %copy-start.16 = (f32[256,2]{0,1:T(2,128)S(1)}, f32[256,2]{0,1:T(2,128)}, u32[]{:S(2)}) copy-start(f32[256,2]{0,1:T(2,128)} %param.45) | copy-start | bytes 6148
  2.1 206.6 %copy-start = (f32[3,3,64,512]{3,2,1,0:T(8,128)S(1)}, f32[3,3,64,512]{3,2,1,0:T(8,128)}, u32[]{:S(2)}) copy-start(f32[3,3,64,512]{3,2,1,0:T(8,128)} %param.34) | copy-start | bytes 3538948
  2.1 206.6 %copy-start.3 = (f32[3,3,64,512]{3,2,1,0:T(8,128)S(1)}, f32[3,3,64,512]{3,2,1,0:T(8,128)}, u32[]{:S(2)}) copy-start(f32[3,3,64,512]{3,2,1,0:T(8,128)} %param.35) | copy-start | bytes 3538948
  208.8 4.3 %copy-start.1 = (f32[3,3,64,256]{3,2,1,0:T(8,128)S(1)}, f32[3,3,64,256]{3,2,1,0:T(8,128)}, u32[]{:S(2)}) copy-start(f32[3,3,64,256]{3,2,1,0:T(8,128)} %param.40) | copy-start | bytes 1769476
  208.8 4.3 %copy-start.5 = (f32[3,3,64,256]{3,2,1,0:T(8,128)S(1)}, f32[3,3,64,256]{3,2,1,0:T(8,128)}, u32[]{:S(2)}) copy-start(f32[3,3,64,256]{3,2,1,0:T(8,128)} %param.41) | copy-start | bytes 1769476
  208.8 4.3 %copy-start.6 = (f32[3,3,64,256]{3,2,1,0:T(8,128)S(1)}, f32[3,3,64,256]{3,2,1,0:T(8,128)}, u32[]{:S(2)}) copy-start(f32[3,3,64,256]{3,2,1,0:T(8,128)} %param.42) | copy-start | bytes 1769476
  208.8 4.3 %copy-start.7 = (f32[9,64,256]{2,1,0:T(8,128)S(1)}, f32[9,64,256]{2,1,0:T(8,128)}, u32[]{:S(2)}) copy-start(f32[9,64,256]{2,1,0:T(8,128)} %get-tuple-element.30) | copy-start | bytes 1769476
  213.1 1.7 copy-start.2
  213.1 1.6 copy-start.8
  213.1 2.1 copy-start.9
  213.1 2.2 %copy-start.10 = (bf16[9,32,512]{2,1,0:T(8,128)(2,1)S(1)}, bf16[9,32,512]{2,1,0:T(8,128)(2,1)}, u32[]{:S(2)}) copy-start(bf16[9,32,512]{2,1,0:T(8,128)(2,1)} %get-tuple-element.27) | copy-start | bytes 884740
  215.3 1.7 copy-start.4
  215.3 1.7 copy-start.11
  215.3 1.7 copy-start.12
  215.3 1.7 copy-start.13

commit v4 on v3

--- a/solution.py
+++ b/solution.py
@@ -358,6 +358,7 @@
     ("lab", (8, 128), F32),
     ("flat", (4, 256, 128), F32),
     ("w1", (9, 32, 512), BF),
+    ("S1", (9, 32, 512), BF),
     ("w2", (9, 64, 512), BF),
     ("wu", (4, 64, 256), BF),
     ("w3", (9, 64, 256), BF),
@@ -392,6 +393,7 @@
     ("act3", (64, 2048), BF),
     ("LG", (8, 32, 128), F32),
     ("LBL", (32, 128), F32),
+    ("HT", (256, 8), F32),
     ("DL", (32, 128), F32),
     ("G3", (4, 8, 64, 512), BF),
     ("Z", (1152, 2048), F32),
@@ -419,7 +421,7 @@
     ("RG1", (9, 32, 512), BF),
     ("HD", (16, 8, 128), F32),
 )
-COPIES = 216
+COPIES = 224
 
 
 def fused(widths, *refs):
@@ -462,9 +464,12 @@
         count[0] += n
         return base
 
-    def hand(src, dst, h2, y2, sem_s, sem_r):
+    def hand(src, dst, h2, y2, sem_s, sem_r, needed=None):
         same = jnp.logical_and(h2 == h, y2 == y)
         away = jnp.logical_not(same)
+        if needed is not None:
+            same = jnp.logical_and(same, needed)
+            away = jnp.logical_and(away, needed)
         copy = remote(src, dst, h2, y2, sem_s, sem_r)
 
         @pl.when(same)
@@ -511,23 +516,6 @@
         flat[c, 0:wa, :] = rows_a[:, half].astype(F32)
         flat[c, wa : wa + wb, :] = rows_b[:, half].astype(F32)
         inT[c] = flat[c, 0:128, :].T.astype(BF).reshape(4, 32, 128)
-    w1[...] = f1[...].astype(BF)
-    place = lax.broadcasted_iota(jnp.int32, (256, LANE), 0)
-    lane = lax.broadcasted_iota(jnp.int32, (256, LANE), 1)
-    spread = jnp.concatenate(
-        [
-            jnp.concatenate([first[...], second[...]], axis=1).astype(F32)
-            for first, second in ((la, lb), (va, vb))
-        ],
-        axis=0,
-    )
-    spread = jnp.pad(spread, ((0, 4), (0, 256 - wide_a - wide_b)))
-    for b in range(2):
-        pick = jnp.where(place == 2 * lane + b, 1.0, 0.0)
-        planes = dot_nn(spread.astype(BF), pick.astype(BF))
-        for a in range(2):
-            lab[2 * a + b : 2 * a + b + 1, :] = planes[a : a + 1, :]
-            lab[4 + 2 * a + b : 5 + 2 * a + b, :] = planes[2 + a : 3 + a, :]
 
     IN, LB = m["IN"], m["LB"]
     in_copies = []
@@ -548,21 +536,60 @@
     IN[2 * z + x, e, pl.ds(2 * y, 2)] = inT[:, 2 * x + y]
 
     W1, W2, WU, W3 = m["W1"], m["W2"], m["WU"], m["W3"]
+    w1[...] = f1[...].astype(BF)
+    S1 = m["S1"]
+    near = e == y
     b1 = reserve(4)
-    for i in range(4):
-        hand(
-            w1.at[:, :, i * 128 : i * 128 + 128],
-            W1.at[:, span(z, 32), :],
-            ha(2 * y + i // 2, x, i % 2),
-            e,
-            b1 + i,
-            b1 + z,
-        )
+    b1s = reserve(5)
+    over = remote(w1, S1, h, 1 - y, b1s + 4, b1s + 4)
+
+    @pl.when(jnp.logical_not(near))
+    def _():
+        over.start()
+
+    started.append((over, jnp.logical_not(near)))
+
+    def spread_first(shard, half, base):
+        for k in range(4):
+            i = lax.rem(k + 2 * lax.rem(z, 2), 4)
+            hand(
+                shard.at[:, :, span(i, 128)],
+                W1.at[:, span(z, 32), :],
+                ha(2 * half + lax.div(i, 2), x, lax.rem(i, 2)),
+                e,
+                base + k,
+                b1 + z,
+                near,
+            )
+
+    spread_first(w1, y, b1)
+    place = lax.broadcasted_iota(jnp.int32, (256, LANE), 0)
+    lane = lax.broadcasted_iota(jnp.int32, (256, LANE), 1)
+    spread = jnp.concatenate(
+        [
+            jnp.concatenate([first[...], second[...]], axis=1).astype(F32)
+            for first, second in ((la, lb), (va, vb))
+        ],
+        axis=0,
+    )
+    spread = jnp.pad(spread, ((0, 4), (0, 256 - wide_a - wide_b)))
+    for b in range(2):
+        pick = jnp.where(place == 2 * lane + b, 1.0, 0.0)
+        planes = dot_nn(spread.astype(BF), pick.astype(BF))
+        for a in range(2):
+            lab[2 * a + b : 2 * a + b + 1, :] = planes[a : a + 1, :]
+            lab[4 + 2 * a + b : 5 + 2 * a + b, :] = planes[2 + a : 3 + a, :]
     lab_copies = []
     LB[h] = lab[...]
     for d in range(1, 16):
         lab_copies.append(push(lab, LB.at[h], lax.rem(h + d, 16), y))
 
+
+    @pl.when(near)
+    def _():
+        over.wait_recv()
+
+    spread_first(S1, 1 - y, b1s)
     for copy in in_copies:
         copy.wait_recv()
     twin_in = push(IN.at[:, e], IN.at[:, e], twin, y)
@@ -609,7 +636,7 @@
         hand(
             w3,
             W3.at[:, span(lax.div(z, 2), 64), span(y, 256)],
-            ha(i, x, e),
+            ha(lax.rem(z + i, 4), x, e),
             lax.rem(z, 2),
             b3 + i,
             b3 + 2 * lax.div(z, 2) + y,
@@ -879,7 +906,9 @@
     pair_three(3)
     pre3, act3, LG = m["pre3"], m["act3"], m["LG"]
     wide = (64, LANE)
-    head = fh[span(slot, 64), :].astype(BF).astype(F32)
+    turned = jnp.concatenate([fh[...], jnp.zeros((6, fh.shape[1]), F32)], axis=0).T
+    m["HT"][...] = turned.astype(BF).astype(F32)
+    head = m["HT"][span(slot, 64), :]
     h0 = jnp.broadcast_to(head[:, 0:1], wide)
     h1 = jnp.broadcast_to(head[:, 1:2], wide)
     for b in range(16):
@@ -960,12 +989,44 @@
         grads = G3[p].reshape(512, 512)
         Z[0:576, p * 512 : p * 512 + 512] = dot_nn(W3[:, 0:64, :].reshape(576, 512), grads)
 
-    passes = [plane_passes(G3.at[0], planes[0])]
+    GW3, GWU, GW2, GW1 = m["GW3"], m["GWU"], m["GW2"], m["GW1"]
+    RG3, RGU, RG2, RG1 = m["RG3"], m["RGU"], m["RG2"], m["RG1"]
+
+    def grad_three(p):
+        def step(t, carry):
+            part = dot_nt(X[span(t, 128), 128 + p * 512 : 640 + p * 512], G3[p].reshape(512, 512))
+            rows = pl.ds(pl.multiple_of(576 + 128 * lax.div(t, 4), 64), 128)
+            cols = span(lax.rem(t, 4), 512)
+            if p > 0:
+                part = part + Z[rows, cols]
+            if p < 3:
+                Z[rows, cols] = part
+            else:
+                GW3[t] = part.astype(BF)
+            return carry
+
+        lax.fori_loop(0, 9, step, 0)
+
+    passes = plane_passes(G3.at[0], planes[0])
     for p in range(4):
+        arrive(passes)
+        back_three(p)
         if p < 3:
-            passes.append(plane_passes(G3.at[p + 1], planes[p + 1]))
-        arrive(passes[p])
-        back_three(p)
+            passes = plane_passes(G3.at[p + 1], planes[p + 1])
+            grad_three(p)
+    def merge_home(first, last):
+        for k in range(first, last):
+            half, own = lax.rem(y + k // 2, 2), k < 2
+            t = lax.rem(lax.div(z, 2) + 1 + k, 2)
+            hand(
+                GW3.at[:, span(t, 64), span(y, 256)] if own else m["Y3"].at[t],
+                RG3.at[z],
+                ha(2 * t + half, x, e),
+                y,
+                bg3 + k,
+                bg3 + z,
+            )
+
     ways = (((0, 0, 0), (1, -1, 0), (1, 1, 1)), ((0, -1, -1), (0, 1, 0), (1, 0, 0)))
 
     def raised_block(a, b, i):
@@ -996,18 +1057,9 @@
                     DB[p] = block
                 else:
                     DR[p * 64 : p * 64 + 64, i * 128 : i * 128 + 128] = block.astype(BF)
-    GW3, GWU, GW2, GW1 = m["GW3"], m["GWU"], m["GW2"], m["GW1"]
-    RG3, RGU, RG2, RG1 = m["RG3"], m["RGU"], m["RG2"], m["RG1"]
-
-    def grad_three(t, carry):
-        total = None
-        for p in range(4):
-            part = dot_nt(X[span(t, 128), 128 + p * 512 : 640 + p * 512], G3[p].reshape(512, 512))
-            total = part if total is None else total + part
-        GW3[t] = total.astype(BF)
-        return carry
-
-    lax.fori_loop(0, 3, grad_three, 0)
+    grad_three(3)
+    bg3 = reserve(4)
+    merge_home(0, 2)
     wait_fringe()
     for a in range(2):
         for b in range(2):
@@ -1031,28 +1083,14 @@
             Z[span(2 * k + e, 128), 0:512] = total
             S7b[k] = total.astype(BF)
 
-    lax.fori_loop(3, 5, grad_three, 0)
     wait_pair.wait_recv()
     pair_seven()
     wait_seven = scatter(S7b, R7)
-    lax.fori_loop(5, 9, grad_three, 0)
 
     def grad_up(k, carry):
         GWU[pl.ds(2 * k, 2)] = dot_nt(A2[k], DR[...]).astype(BF).reshape(2, 64, 256)
         return carry
 
-    lax.fori_loop(0, 8, grad_up, 0)
-    arrive(wait_seven)
-    G2 = m["G2"]
-    total = Z[span(s, 128), 0:512] + R7[0].astype(F32)
-    total = total + R7[1].astype(F32) + R7[2].astype(F32)
-    G2[e, :, span(z, 512)] = (total * gelu_slope(pre2[...])).astype(BF)
-    mine = G2.at[e, :, span(z, 512)]
-    g2_copies = []
-    for d in range(1, 4):
-        zt = lax.rem(z + d, 4)
-        g2_copies.append(push(mine, mine, ha(zt, x, e), y))
-    own_pair = push(mine, mine, twin, y)
     Y3 = m["Y3"]
     other = 1 - y
     across = []
@@ -1065,8 +1103,26 @@
                 other,
             )
         )
+
+    lax.fori_loop(0, 8, grad_up, 0)
     patches(middle_block, 0, 16)
     patch_edges()
+    gu_copies = []
+    for d in range(1, 16):
+        ht = lax.rem(h + d, 16)
+        gu_copies.append(push(GWU.at[ht], RGU.at[h], ht, y))
+    RGU[h] = GWU[h]
+    arrive(wait_seven)
+    G2 = m["G2"]
+    total = Z[span(s, 128), 0:512] + R7[0].astype(F32)
+    total = total + R7[1].astype(F32) + R7[2].astype(F32)
+    G2[e, :, span(z, 512)] = (total * gelu_slope(pre2[...])).astype(BF)
+    mine = G2.at[e, :, span(z, 512)]
+    g2_copies = []
+    for d in range(1, 4):
+        zt = lax.rem(z + d, 4)
+        g2_copies.append(push(mine, mine, ha(zt, x, e), y))
+    own_pair = push(mine, mine, twin, y)
 
     def back_two(zs):
         for k in range(2):
@@ -1079,6 +1135,8 @@
         came = G2.at[e, :, span(zs, 512)]
         return zs, push(came, came, twin, y)
 
+    arrive(across)
+    merge_home(2, 4)
     zs, copy = relay(1)
     own_pair.wait_recv()
     back_two(z)
@@ -1087,21 +1145,6 @@
         copy.wait_recv()
         back_two(zs)
         zs, copy = after
-    bg3 = reserve(4)
-    for t in range(2):
-        hand(
-            GW3.at[:, 64 * t : 64 * t + 64, span(y, 256)],
-            RG3.at[z],
-            ha(2 * t + y, x, e),
-            y,
-            bg3 + t,
-            bg3 + z,
-        )
-    gu_copies = []
-    for d in range(1, 16):
-        ht = lax.rem(h + d, 16)
-        gu_copies.append(push(GWU.at[ht], RGU.at[h], ht, y))
-    RGU[h] = GWU[h]
     copy.wait_recv()
     back_two(zs)
     P8b, R8, G1 = m["P8b"], m["R8"], m["G1"]
@@ -1128,16 +1171,6 @@
     for c in range(2):
         lax.fori_loop(8 * c, 8 * c + 8, fold, 0)
         wait_eight.append(scatter(P8b, R8, halves[c]))
-    arrive(across)
-    for t in range(2):
-        hand(
-            Y3.at[t],
-            RG3.at[z],
-            ha(2 * t + other, x, e),
-            y,
-            bg3 + 2 + t,
-            bg3 + z,
-        )
 
     def grad_two(t, carry):
         GW2[t] = dot_nt(X[span(t, 128), 128:2176], G2[...].reshape(256, 2048)).astype(BF)
@@ -1178,13 +1211,14 @@
     lax.fori_loop(0, 9, grad_one, 0)
     bg1 = reserve(4)
     r_low = 2 * lax.rem(z, 2) + e
-    for j in range(4):
+    for k in range(4):
+        j = lax.rem(z + 1 + k, 4)
         hand(
-            GW1.at[:, 32 * j : 32 * j + 32, :],
+            GW1.at[:, span(j, 32), :],
             RG1.at[:, :, span(r_low, 128)],
             ha(j, x, y),
             lax.div(z, 2),
-            bg1 + j,
+            bg1 + k,
             bg1 + r_low,
         )
 
@@ -1277,22 +1311,97 @@
         w_middle.reshape(9, 64, 512),
         w_upward.reshape(4, 64, 256),
         w_merge.reshape(9, 64, 256),
-        w_head,
-    )
-    grad_enter = g1.astype(F32).reshape(w_enter.shape)
-    grad_middle = g2.astype(F32).reshape(w_middle.shape)
-    grad_upward = gu.reshape(w_upward.shape)
-    grad_merge = g3.reshape(w_merge.shape)
-    grad_head = hd[0:4, 0:2, 0:64].transpose(0, 2, 1).reshape(w_head.shape)
+        w_head.T,
+    )
+    states = (
+        (w_enter, moment_enter, square_enter),
+        (w_middle, moment_middle, square_middle),
+        (w_upward, moment_upward, square_upward),
+        (w_merge, moment_merge, square_merge),
+    )
+    dims = tuple(g.shape for g in (g1, g2, gu, g3))
+    flat = [part.reshape(dim) for dim, state in zip(dims, states) for part in state]
+    anywhere = pl.BlockSpec(memory_space=pltpu.HBM)
+    rows = w_head.T.shape
+    new = pl.pallas_call(
+        updates,
+        out_shape=tuple(
+            jax.ShapeDtypeStruct(dim, kind) for dim in (*dims, rows) for kind in (F32, F32, F32, BF)
+        ),
+        in_specs=[anywhere] * 16 + [vmem] * 4,
+        out_specs=[anywhere] * 16 + [vmem] * 4,
+        scratch_shapes=[
+            pltpu.VMEM(dim, kind)
+            for dim, g in zip(dims, (g1, g2, gu, g3))
+            for kind in (g.dtype, F32, F32, F32, F32, F32, F32, BF)
+        ]
+        + [pltpu.SemaphoreType.DMA((len(PIECES), 8))],
+        compiler_params=pltpu.CompilerParams(vmem_limit_bytes=62 * 1024 * 1024),
+    )(g1, g2, gu, g3, *flat, hd, w_head.T, moment_head.T, square_head.T)
+    shapes = (w_enter.shape, w_middle.shape, w_upward.shape, w_merge.shape)
     return (
-        *adamw(w_enter, moment_enter, square_enter, grad_enter),
-        *adamw(w_middle, moment_middle, square_middle, grad_middle),
-        *adamw(w_upward, moment_upward, square_upward, grad_upward),
-        *adamw(w_merge, moment_merge, square_merge, grad_merge),
-        *adamw(w_head, moment_head, square_head, grad_head),
+        *[new[k].reshape(shapes[k // 4]) for k in range(16)],
+        *[part.T for part in new[16:]],
         hd[0, 2, 0],
         hd[4, 0, 0],
     )
+
+
+PIECES = ((3, 0, 5), (3, 5, 9), (2, 0, 4), (1, 0, 3), (1, 3, 6), (1, 6, 9), (0, 0, 5), (0, 5, 9))
+
+
+def adamw_step(master, moment, square, gradient):
+    moment_new = BETA_ONE * moment + (1.0 - BETA_ONE) * gradient
+    square_new = BETA_TWO * square + (1.0 - BETA_TWO) * gradient * gradient
+    fixed_moment = moment_new * (RATE / (1.0 - BETA_ONE**STEP))
+    fixed_square = square_new * (1.0 / (1.0 - BETA_TWO**STEP))
+    master_new = (1.0 - RATE * DECAY) * master - fixed_moment / (jnp.sqrt(fixed_square) + EPSILON)
+    return (master_new, moment_new, square_new, master_new.astype(BF))
+
+
+def updates(*refs):
+    grads, states = refs[0:4], refs[4:16]
+    hd, head, moment, square = refs[16:20]
+    outs, tiny = refs[20:36], refs[36:40]
+    held, sems = refs[40:72], refs[72]
+
+    def copies(piece):
+        k, first, last = PIECES[piece]
+        at = slice(first, last)
+        inward = [
+            pltpu.make_async_copy(source.at[at], held[8 * k + j].at[at], sems.at[piece, j])
+            for j, source in enumerate((grads[k], *states[3 * k : 3 * k + 3]))
+        ]
+        outward = [
+            pltpu.make_async_copy(held[8 * k + 4 + j].at[at], outs[4 * k + j].at[at], sems.at[piece, 4 + j])
+            for j in range(4)
+        ]
+        return inward, outward
+
+    every = [copies(piece) for piece in range(len(PIECES))]
+    for inward, _ in every:
+        for copy in inward:
+            copy.start()
+    gradient = jnp.concatenate([hd[j, 0:2, 0:64] for j in range(4)], axis=1)
+    for ref, value in zip(tiny, adamw_step(head[...], moment[...], square[...], gradient)):
+        ref[...] = value
+    for (k, first, last), (inward, outward) in zip(PIECES, every):
+        for copy in inward:
+            copy.wait()
+        own = held[8 * k : 8 * k + 8]
+
+        def step(i, carry, own=own):
+            made = adamw_step(own[1][i], own[2][i], own[3][i], own[0][i].astype(F32))
+            for ref, value in zip(own[4:], made):
+                ref[i] = value
+            return carry
+
+        lax.fori_loop(first, last, step, 0)
+        for copy in outward:
+            copy.start()
+    for _, outward in every:
+        for copy in outward:
+            copy.wait()
 
 
 def chosen(*args):

time: 220 us -> 216 us (0.982)
  other arithmetic: 9.14 us -> 0 us
  Pallas kernels: 205 us -> 214 us
  local copies, waits for them, and re-layouts: 4.16 us -> 1.2 us
    convert_element_type x5 -> x0, other arithmetic: 9.14 us -> none  [adamw(): return (master_new, moment_new, square_new, master_new.astype(jnp.bfloat16))]
    pallas_call x0 -> x1, Pallas kernels: none -> 9.08 us  [resident_body(): pl.pallas_call(updates, out_shape=tuple((jax.ShapeDtypeStruct(dim, kind)...]
where the time goes in v4:
time: 216 us
  Pallas kernels  214 us (99%)
    pallas_call x1, Pallas kernels, resident_body(): pl.pallas_call(lambda *refs: fused((input_a.shape[2], input_b.shape[2]),...  205 us
    pallas_call x1, Pallas kernels, resident_body(): pl.pallas_call(updates, out_shape=tuple((jax.ShapeDtypeStruct(dim, kind)...  9.08 us

profile of v4, /device:TPU:14, one launch (start us, length us, event | category | flops | bytes accessed | tf_op | source)
XLA Modules:
  0.0 215.9 jit_solution(10254596362573628550)
XLA Ops:
  0.7 204.9 %shard_map.390 = (bf16[9,32,512]{2,1,0:T(8,128)(2,1)}, bf16[9,64,512]{2,1,0:T(8,128)(2,1)}, f32[4,64,256]{2,1,0:T(8,128)}, f32[9,64,256]{2,1,0:T(8,128)}, f32[5,8,128]{2,1,0:T(8,128)}) custom-call(bf16[48,256]{1,0:T(8,128)(2,1)} %bitcast.64, bf16[72,256]{1,0:T(8,128)(2,1)} %bitcast.63, bf16[2,96,256]{2,1,0:T(8,128)(2,1)} %bitcast.62, ...), custom_call_target="tpu_custom_call" | custom-call | tf_op jit(solution)/shard_map/pallas_call | solution.py:1285
  205.6 9.1 %shard_map.391 = (f32[9,32,512]{2,1,0:T(8,128)}, f32[9,32,512]{2,1,0:T(8,128)}, f32[9,32,512]{2,1,0:T(8,128)}, bf16[9,32,512]{2,1,0:T(8,128)(2,1)}, f32[9,64,512...) custom-call(bf16[9,32,512]{2,1,0:T(8,128)(2,1)} %get-tuple-element.4, ...), custom_call_target="tpu_custom_call" | custom-call | tf_op jit(solution)/shard_map/pallas_call | solution.py:1326
  214.7 1.2 fusion

commit v5 on v4

--- a/solution.py
+++ b/solution.py
@@ -435,6 +435,15 @@
     q = 2 * y + x
     s = 2 * q + e
     twin = h + 1 - 2 * e
+    entered = pltpu.get_barrier_semaphore()
+    for d in range(16):
+        for side in (y, 1 - y)[0 if d else 1 :]:
+            pl.semaphore_signal(
+                entered,
+                inc=1,
+                device_id={"ha": lax.rem(h + d, 16), "col": side},
+                device_id_type=MESH,
+            )
     started = []
     count = [0]
 
@@ -516,6 +525,9 @@
         flat[c, 0:wa, :] = rows_a[:, half].astype(F32)
         flat[c, wa : wa + wb, :] = rows_b[:, half].astype(F32)
         inT[c] = flat[c, 0:128, :].T.astype(BF).reshape(4, 32, 128)
+
+    w1[...] = f1[...].astype(BF)
+    pl.semaphore_wait(entered, 31)
 
     IN, LB = m["IN"], m["LB"]
     in_copies = []
@@ -536,7 +548,6 @@
     IN[2 * z + x, e, pl.ds(2 * y, 2)] = inT[:, 2 * x + y]
 
     W1, W2, WU, W3 = m["W1"], m["W2"], m["WU"], m["W3"]
-    w1[...] = f1[...].astype(BF)
     S1 = m["S1"]
     near = e == y
     b1 = reserve(4)
@@ -1296,7 +1307,7 @@
         scratch_shapes=[pltpu.VMEM(shape, kind) for _, shape, kind in SCRATCH]
         + [pltpu.SemaphoreType.DMA((COPIES,)), pltpu.SemaphoreType.DMA((COPIES,))],
         compiler_params=pltpu.CompilerParams(
-            has_side_effects=True, vmem_limit_bytes=56 * 1024 * 1024
+            collective_id=0, has_side_effects=True, vmem_limit_bytes=56 * 1024 * 1024
         ),
     )(
         input_a[0, 0],

time: 216 us -> 210 us (0.972)
  Pallas kernels: 214 us -> 208 us
    pallas_call x1, Pallas kernels: 205 us -> 199 us  [resident_body(): pl.pallas_call(lambda *refs: fused((input_a.shape[2], input_b.shape[2]),...]
where the time goes in v5:
time: 210 us
  Pallas kernels  208 us (99%)
    pallas_call x1, Pallas kernels, resident_body(): pl.pallas_call(lambda *refs: fused((input_a.shape[2], input_b.shape[2]),...  199 us
    pallas_call x1, Pallas kernels, resident_body(): pl.pallas_call(updates, out_shape=tuple((jax.ShapeDtypeStruct(dim, kind)...  9.08 us

profile of v5, /device:TPU:14, one launch (start us, length us, event | category | flops | bytes accessed | tf_op | source)
XLA Modules:
  0.0 209.9 jit_solution(3070088805956900016)
XLA Ops:
  0.7 199.0 %shard_map.390 = (bf16[9,32,512]{2,1,0:T(8,128)(2,1)}, bf16[9,64,512]{2,1,0:T(8,128)(2,1)}, f32[4,64,256]{2,1,0:T(8,128)}, f32[9,64,256]{2,1,0:T(8,128)}, f32[5,8,128]{2,1,0:T(8,128)}) custom-call(bf16[48,256]{1,0:T(8,128)(2,1)} %bitcast.64, bf16[72,256]{1,0:T(8,128)(2,1)} %bitcast.63, bf16[2,96,256]{2,1,0:T(8,128)(2,1)} %bitcast.62, ...), custom_call_target="tpu_custom_call" | custom-call | tf_op jit(solution)/shard_map/pallas_call | solution.py:1296
  199.7 9.1 %shard_map.391 = (f32[9,32,512]{2,1,0:T(8,128)}, f32[9,32,512]{2,1,0:T(8,128)}, f32[9,32,512]{2,1,0:T(8,128)}, bf16[9,32,512]{2,1,0:T(8,128)(2,1)}, f32[9,64,512...) custom-call(bf16[9,32,512]{2,1,0:T(8,128)(2,1)} %get-tuple-element.4, ...), custom_call_target="tpu_custom_call" | custom-call | tf_op jit(solution)/shard_map/pallas_call | solution.py:1337
  208.7 1.2 fusion

commit v6 on v5

--- a/solution.py
+++ b/solution.py
@@ -356,6 +356,9 @@
     ("inT", (2, 4, 32, 128), BF),
     ("skT", (4, 64, 512), BF),
     ("lab", (8, 128), F32),
+    ("F2", (9, 64, 512), F32),
+    ("F3", (9, 64, 256), F32),
+    ("FU", (4, 64, 256), F32),
     ("flat", (4, 256, 128), F32),
     ("w1", (9, 32, 512), BF),
     ("S1", (9, 32, 512), BF),
@@ -428,8 +431,15 @@
     wa, wb = widths
     rows_a, rows_b, skip_a, skip_b, la, lb, va, vb, f1, f2, fu, f3, fh = refs[:13]
     g1o, g2o, guo, g3o, hdo = refs[13:18]
-    m = {name: ref for (name, _, _), ref in zip(SCRATCH, refs[18:-2])}
-    send_sem, recv_sem = refs[-2:]
+    m = {name: ref for (name, _, _), ref in zip(SCRATCH, refs[18:-3])}
+    send_sem, recv_sem, load_sem = refs[-3:]
+    loads = [
+        pltpu.make_async_copy(source, m[name], load_sem.at[n])
+        for n, (source, name) in enumerate(((f2, "F2"), (f3, "F3"), (fu, "FU")))
+    ]
+    for load in loads:
+        load.start()
+    f2, f3, fu = m["F2"], m["F3"], m["FU"]
     h, y = lax.axis_index("ha"), lax.axis_index("col")
     z, x, e = lax.div(h, 4), lax.rem(lax.div(h, 2), 2), lax.rem(h, 2)
     q = 2 * y + x
@@ -530,6 +540,32 @@
     pl.semaphore_wait(entered, 31)
 
     IN, LB = m["IN"], m["LB"]
+    W1, W2, WU, W3 = m["W1"], m["W2"], m["WU"], m["W3"]
+    S1 = m["S1"]
+    near = e == y
+    b1 = reserve(4)
+    b1s = reserve(5)
+    over = remote(w1, S1, h, 1 - y, b1s + 4, b1s + 4)
+
+    @pl.when(jnp.logical_not(near))
+    def _():
+        over.start()
+
+    started.append((over, jnp.logical_not(near)))
+
+    def spread_first(shard, half, base):
+        for k in range(4):
+            i = lax.rem(k + 2 * lax.rem(z, 2), 4)
+            hand(
+                shard.at[:, :, span(i, 128)],
+                W1.at[:, span(z, 32), :],
+                ha(2 * half + lax.div(i, 2), x, lax.rem(i, 2)),
+                e,
+                base + k,
+                b1 + z,
+                near,
+            )
+
     in_copies = []
     for dz in range(4):
         zt = lax.rem(z + dz, 4)
@@ -547,32 +583,6 @@
             )
     IN[2 * z + x, e, pl.ds(2 * y, 2)] = inT[:, 2 * x + y]
 
-    W1, W2, WU, W3 = m["W1"], m["W2"], m["WU"], m["W3"]
-    S1 = m["S1"]
-    near = e == y
-    b1 = reserve(4)
-    b1s = reserve(5)
-    over = remote(w1, S1, h, 1 - y, b1s + 4, b1s + 4)
-
-    @pl.when(jnp.logical_not(near))
-    def _():
-        over.start()
-
-    started.append((over, jnp.logical_not(near)))
-
-    def spread_first(shard, half, base):
-        for k in range(4):
-            i = lax.rem(k + 2 * lax.rem(z, 2), 4)
-            hand(
-                shard.at[:, :, span(i, 128)],
-                W1.at[:, span(z, 32), :],
-                ha(2 * half + lax.div(i, 2), x, lax.rem(i, 2)),
-                e,
-                base + k,
-                b1 + z,
-                near,
-            )
-
     spread_first(w1, y, b1)
     place = lax.broadcasted_iota(jnp.int32, (256, LANE), 0)
     lane = lax.broadcasted_iota(jnp.int32, (256, LANE), 1)
@@ -605,6 +615,8 @@
         copy.wait_recv()
     twin_in = push(IN.at[:, e], IN.at[:, e], twin, y)
 
+    for load in loads:
+        load.wait()
     w2[...] = f2[...].astype(BF)
     w3[...] = f3[...].astype(BF)
     for k in range(4):
@@ -1293,6 +1305,7 @@
     square_head,
 ):
     vmem = pl.BlockSpec(memory_space=pltpu.VMEM)
+    anywhere = pl.BlockSpec(memory_space=pl.ANY)
     g1, g2, gu, g3, hd = pl.pallas_call(
         lambda *refs: fused((input_a.shape[2], input_b.shape[2]), *refs),
         out_shape=(
@@ -1302,12 +1315,12 @@
             jax.ShapeDtypeStruct((9, 64, 256), F32),
             jax.ShapeDtypeStruct((5, 8, 128), F32),
         ),
-        in_specs=[vmem] * 13,
+        in_specs=[vmem] * 9 + [anywhere] * 3 + [vmem],
         out_specs=[vmem] * 5,
         scratch_shapes=[pltpu.VMEM(shape, kind) for _, shape, kind in SCRATCH]
-        + [pltpu.SemaphoreType.DMA((COPIES,)), pltpu.SemaphoreType.DMA((COPIES,))],
+        + [pltpu.SemaphoreType.DMA((COPIES,)), pltpu.SemaphoreType.DMA((COPIES,)), pltpu.SemaphoreType.DMA((3,))],
         compiler_params=pltpu.CompilerParams(
-            collective_id=0, has_side_effects=True, vmem_limit_bytes=56 * 1024 * 1024
+            collective_id=0, has_side_effects=True, vmem_limit_bytes=61 * 1024 * 1024
         ),
     )(
         input_a[0, 0],
@@ -1332,15 +1345,15 @@
     )
     dims = tuple(g.shape for g in (g1, g2, gu, g3))
     flat = [part.reshape(dim) for dim, state in zip(dims, states) for part in state]
-    anywhere = pl.BlockSpec(memory_space=pltpu.HBM)
     rows = w_head.T.shape
     new = pl.pallas_call(
         updates,
         out_shape=tuple(
             jax.ShapeDtypeStruct(dim, kind) for dim in (*dims, rows) for kind in (F32, F32, F32, BF)
-        ),
+        )
+        + (jax.ShapeDtypeStruct((1, 1), F32),) * 2,
         in_specs=[anywhere] * 16 + [vmem] * 4,
-        out_specs=[anywhere] * 16 + [vmem] * 4,
+        out_specs=[anywhere] * 16 + [vmem] * 6,
         scratch_shapes=[
             pltpu.VMEM(dim, kind)
             for dim, g in zip(dims, (g1, g2, gu, g3))
@@ -1352,9 +1365,9 @@
     shapes = (w_enter.shape, w_middle.shape, w_upward.shape, w_merge.shape)
     return (
         *[new[k].reshape(shapes[k // 4]) for k in range(16)],
-        *[part.T for part in new[16:]],
-        hd[0, 2, 0],
-        hd[4, 0, 0],
+        *[part.T for part in new[16:20]],
+        new[20].reshape(()),
+        new[21].reshape(()),
     )
 
 
@@ -1373,8 +1386,8 @@
 def updates(*refs):
     grads, states = refs[0:4], refs[4:16]
     hd, head, moment, square = refs[16:20]
-    outs, tiny = refs[20:36], refs[36:40]
-    held, sems = refs[40:72], refs[72]
+    outs, tiny, loss, labelled = refs[20:36], refs[36:40], refs[40], refs[41]
+    held, sems = refs[42:74], refs[74]
 
     def copies(piece):
         k, first, last = PIECES[piece]
@@ -1393,6 +1406,8 @@
     for inward, _ in every:
         for copy in inward:
             copy.start()
+    loss[...] = hd[0, 2:3, 0:1]
+    labelled[...] = hd[4, 0:1, 0:1]
     gradient = jnp.concatenate([hd[j, 0:2, 0:64] for j in range(4)], axis=1)
     for ref, value in zip(tiny, adamw_step(head[...], moment[...], square[...], gradient)):
         ref[...] = value

time: 210 us -> 208 us (level)
  no operation moved by 1% of the time
where the time goes in v6:
time: 208 us; the launch traced here: 207 us
  Pallas kernels  207 us (100%)
    pallas_call x1, Pallas kernels, resident_body(): pl.pallas_call(lambda *refs: fused((input_a.shape[2], input_b.shape[2]),...  197 us
    pallas_call x1, Pallas kernels, resident_body(): pl.pallas_call(updates, out_shape=tuple((jax.ShapeDtypeStruct(dim, kind)...  9.09 us

profile of v6, /device:TPU:14, one launch (start us, length us, event | category | flops | bytes accessed | tf_op | source)
XLA Modules:
  0.0 207.3 jit_solution(10512448948575304683)
XLA Ops:
  0.7 197.4 %shard_map.390 = (bf16[9,32,512]{2,1,0:T(8,128)(2,1)}, bf16[9,64,512]{2,1,0:T(8,128)(2,1)}, f32[4,64,256]{2,1,0:T(8,128)}, f32[9,64,256]{2,1,0:T(8,128)}, f32[5,8,128]{2,1,0:T(8,128)}) custom-call(bf16[48,256]{1,0:T(8,128)(2,1)} %bitcast.64, bf16[72,256]{1,0:T(8,128)(2,1)} %bitcast.63, bf16[2,96,256]{2,1,0:T(8,128)(2,1)} %bitcast.62, ...), custom_call_target="tpu_custom_call" | custom-call | tf_op jit(solution)/shard_map/pallas_call | solution.py:1309
  198.1 9.1 %shard_map.391 = (f32[9,32,512]{2,1,0:T(8,128)}, f32[9,32,512]{2,1,0:T(8,128)}, f32[9,32,512]{2,1,0:T(8,128)}, bf16[9,32,512]{2,1,0:T(8,128)(2,1)}, f32[9,64,512...) custom-call(bf16[9,32,512]{2,1,0:T(8,128)(2,1)} %get-tuple-element.4, ...), custom_call_target="tpu_custom_call" | custom-call | tf_op jit(solution)/shard_map/pallas_call | solution.py:1349

commit v7 on v6

--- a/solution.py
+++ b/solution.py
@@ -1130,11 +1130,6 @@
     lax.fori_loop(0, 8, grad_up, 0)
     patches(middle_block, 0, 16)
     patch_edges()
-    gu_copies = []
-    for d in range(1, 16):
-        ht = lax.rem(h + d, 16)
-        gu_copies.append(push(GWU.at[ht], RGU.at[h], ht, y))
-    RGU[h] = GWU[h]
     arrive(wait_seven)
     G2 = m["G2"]
     total = Z[span(s, 128), 0:512] + R7[0].astype(F32)
@@ -1146,6 +1141,11 @@
         zt = lax.rem(z + d, 4)
         g2_copies.append(push(mine, mine, ha(zt, x, e), y))
     own_pair = push(mine, mine, twin, y)
+    gu_copies = []
+    for d in range(1, 16):
+        ht = lax.rem(h + d, 16)
+        gu_copies.append(push(GWU.at[ht], RGU.at[h], ht, y))
+    RGU[h] = GWU[h]
 
     def back_two(zs):
         for k in range(2):

time: 208 us -> 205 us (0.986)
  Pallas kernels: 207 us -> 204 us
    pallas_call x1, Pallas kernels: 197 us -> 195 us  [resident_body(): pl.pallas_call(lambda *refs: fused((input_a.shape[2], input_b.shape[2]),...]
where the time goes in v7:
time: 205 us
  Pallas kernels  204 us (100%)
    pallas_call x1, Pallas kernels, resident_body(): pl.pallas_call(lambda *refs: fused((input_a.shape[2], input_b.shape[2]),...  195 us
    pallas_call x1, Pallas kernels, resident_body(): pl.pallas_call(updates, out_shape=tuple((jax.ShapeDtypeStruct(dim, kind)...  9.09 us

profile of v7, /device:TPU:14, one launch (start us, length us, event | category | flops | bytes accessed | tf_op | source)
XLA Modules:
  0.0 204.5 jit_solution(17436528572241697097)
XLA Ops:
  0.7 194.6 %shard_map.390 = (bf16[9,32,512]{2,1,0:T(8,128)(2,1)}, bf16[9,64,512]{2,1,0:T(8,128)(2,1)}, f32[4,64,256]{2,1,0:T(8,128)}, f32[9,64,256]{2,1,0:T(8,128)}, f32[5,8,128]{2,1,0:T(8,128)}) custom-call(bf16[48,256]{1,0:T(8,128)(2,1)} %bitcast.64, bf16[72,256]{1,0:T(8,128)(2,1)} %bitcast.63, bf16[2,96,256]{2,1,0:T(8,128)(2,1)} %bitcast.62, ...), custom_call_target="tpu_custom_call" | custom-call | tf_op jit(solution)/shard_map/pallas_call | solution.py:1309
  195.3 9.1 %shard_map.391 = (f32[9,32,512]{2,1,0:T(8,128)}, f32[9,32,512]{2,1,0:T(8,128)}, f32[9,32,512]{2,1,0:T(8,128)}, bf16[9,32,512]{2,1,0:T(8,128)(2,1)}, f32[9,64,512...) custom-call(bf16[9,32,512]{2,1,0:T(8,128)(2,1)} %get-tuple-element.4, ...), custom_call_target="tpu_custom_call" | custom-call | tf_op jit(solution)/shard_map/pallas_call | solution.py:1349

commit v8 on v7

--- a/solution.py
+++ b/solution.py
@@ -1158,11 +1158,11 @@
         came = G2.at[e, :, span(zs, 512)]
         return zs, push(came, came, twin, y)
 
-    arrive(across)
-    merge_home(2, 4)
     zs, copy = relay(1)
     own_pair.wait_recv()
     back_two(z)
+    arrive(across)
+    merge_home(2, 4)
     for d in range(2, 4):
         after = relay(d)
         copy.wait_recv()

time: 205 us -> 204 us (level)
  no operation moved by 1% of the time
where the time goes in v8:
time: 204 us
  Pallas kernels  203 us (100%)
    pallas_call x1, Pallas kernels, resident_body(): pl.pallas_call(lambda *refs: fused((input_a.shape[2], input_b.shape[2]),...  194 us
    pallas_call x1, Pallas kernels, resident_body(): pl.pallas_call(updates, out_shape=tuple((jax.ShapeDtypeStruct(dim, kind)...  9.09 us

profile of v8, /device:TPU:14, one launch (start us, length us, event | category | flops | bytes accessed | tf_op | source)
XLA Modules:
  0.0 204.0 jit_solution(8565466706756367947)
XLA Ops:
  0.7 194.0 %shard_map.390 = (bf16[9,32,512]{2,1,0:T(8,128)(2,1)}, bf16[9,64,512]{2,1,0:T(8,128)(2,1)}, f32[4,64,256]{2,1,0:T(8,128)}, f32[9,64,256]{2,1,0:T(8,128)}, f32[5,8,128]{2,1,0:T(8,128)}) custom-call(bf16[48,256]{1,0:T(8,128)(2,1)} %bitcast.64, bf16[72,256]{1,0:T(8,128)(2,1)} %bitcast.63, bf16[2,96,256]{2,1,0:T(8,128)(2,1)} %bitcast.62, ...), custom_call_target="tpu_custom_call" | custom-call | tf_op jit(solution)/shard_map/pallas_call | solution.py:1309
  194.7 9.1 %shard_map.391 = (f32[9,32,512]{2,1,0:T(8,128)}, f32[9,32,512]{2,1,0:T(8,128)}, f32[9,32,512]{2,1,0:T(8,128)}, bf16[9,32,512]{2,1,0:T(8,128)(2,1)}, f32[9,64,512...) custom-call(bf16[9,32,512]{2,1,0:T(8,128)(2,1)} %get-tuple-element.4, ...), custom_call_target="tpu_custom_call" | custom-call | tf_op jit(solution)/shard_map/pallas_call | solution.py:1349

commit v9 on v8

--- a/solution.py
+++ b/solution.py
@@ -1141,28 +1141,28 @@
         zt = lax.rem(z + d, 4)
         g2_copies.append(push(mine, mine, ha(zt, x, e), y))
     own_pair = push(mine, mine, twin, y)
+
+    def back_two(zs):
+        for k in range(2):
+            cols = pl.ds(pl.multiple_of(zs * 512 + k * 256, 256), 256)
+            Z[:, cols] = dot_nn(W2[...].reshape(1152, 256), G2[:, :, cols].reshape(256, 256))
+
+    def relay(d):
+        g2_copies[d - 1].wait_recv()
+        zs = lax.rem(z + 4 - d, 4)
+        came = G2.at[e, :, span(zs, 512)]
+        return zs, push(came, came, twin, y)
+
+    zs, copy = relay(1)
+    own_pair.wait_recv()
+    back_two(z)
+    arrive(across)
+    merge_home(2, 4)
     gu_copies = []
     for d in range(1, 16):
         ht = lax.rem(h + d, 16)
         gu_copies.append(push(GWU.at[ht], RGU.at[h], ht, y))
     RGU[h] = GWU[h]
-
-    def back_two(zs):
-        for k in range(2):
-            cols = pl.ds(pl.multiple_of(zs * 512 + k * 256, 256), 256)
-            Z[:, cols] = dot_nn(W2[...].reshape(1152, 256), G2[:, :, cols].reshape(256, 256))
-
-    def relay(d):
-        g2_copies[d - 1].wait_recv()
-        zs = lax.rem(z + 4 - d, 4)
-        came = G2.at[e, :, span(zs, 512)]
-        return zs, push(came, came, twin, y)
-
-    zs, copy = relay(1)
-    own_pair.wait_recv()
-    back_two(z)
-    arrive(across)
-    merge_home(2, 4)
     for d in range(2, 4):
         after = relay(d)
         copy.wait_recv()

time: 204 us -> 209 us (1.025); the launches traced: 204 us -> 207 us
  Pallas kernels: 203 us -> 206 us
    pallas_call x1, Pallas kernels: 194 us -> 197 us  [resident_body(): pl.pallas_call(lambda *refs: fused((input_a.shape[2], input_b.shape[2]),...]
where the time goes in v9:
time: 209 us; the launch traced here: 207 us
  Pallas kernels  206 us (99%)
    pallas_call x1, Pallas kernels, resident_body(): pl.pallas_call(lambda *refs: fused((input_a.shape[2], input_b.shape[2]),...  197 us
    pallas_call x1, Pallas kernels, resident_body(): pl.pallas_call(updates, out_shape=tuple((jax.ShapeDtypeStruct(dim, kind)...  9.09 us

profile of v9, /device:TPU:14, one launch (start us, length us, event | category | flops | bytes accessed | tf_op | source)
XLA Modules:
  0.0 206.6 jit_solution(16995712577026395101)
XLA Ops:
  0.7 196.6 %shard_map.390 = (bf16[9,32,512]{2,1,0:T(8,128)(2,1)}, bf16[9,64,512]{2,1,0:T(8,128)(2,1)}, f32[4,64,256]{2,1,0:T(8,128)}, f32[9,64,256]{2,1,0:T(8,128)}, f32[5,8,128]{2,1,0:T(8,128)}) custom-call(bf16[48,256]{1,0:T(8,128)(2,1)} %bitcast.64, bf16[72,256]{1,0:T(8,128)(2,1)} %bitcast.63, bf16[2,96,256]{2,1,0:T(8,128)(2,1)} %bitcast.62, ...), custom_call_target="tpu_custom_call" | custom-call | tf_op jit(solution)/shard_map/pallas_call | solution.py:1309
  197.3 9.1 %shard_map.391 = (f32[9,32,512]{2,1,0:T(8,128)}, f32[9,32,512]{2,1,0:T(8,128)}, f32[9,32,512]{2,1,0:T(8,128)}, bf16[9,32,512]{2,1,0:T(8,128)(2,1)}, f32[9,64,512...) custom-call(bf16[9,32,512]{2,1,0:T(8,128)(2,1)} %get-tuple-element.4, ...), custom_call_target="tpu_custom_call" | custom-call | tf_op jit(solution)/shard_map/pallas_call | solution.py:1349
